TPU v7x, 128 devices: a whole 4x4x4 slice. The times are simulated.
128 devices in a mesh: wide: 16 (over y, z), grp: 8 (over x, core).
Axes of the slice: x: 4, y: 4, z: 4, core: 2. Of those that a mesh axis runs over, the one named last changes fastest.
Arguments:
- eta_hat: bfloat16 [2, 2048, 2048], P(None, ('wide', 'grp')), may hold values from -0.0008544922 to 0.0008544922
- phi_hat: bfloat16 [2, 2048, 2048], P(None, ('wide', 'grp')), may hold values from -0.00061035156 to 0.00061035156
- patch_tiles: int32 [256], replicated, may hold values from 0 to 1023, as said below
- fraction: bfloat16 [2, 128, 64, 128, 128], P(None, ('wide', 'grp')), may hold values from 0 to 1
Outputs:
- surface: float32 [2048, 2048], P(('wide', 'grp'))
- fraction_next: bfloat16 [2, 128, 64, 128, 128], P(None, ('wide', 'grp'))
- tendency: float32 [2, 2048, 2048], P(None, ('wide', 'grp'))
Inputs may be any that keep to these rules, and one draw needn't show every extreme that they name: `patch_tiles`: for each g below 8, entries g * 32 to (g + 1) * 32 - 1 are distinct tiles, in ascending order, whose column t % 32 lies in [g * 4, (g + 1) * 4). Of these, the tiles of one band (rows (t // 32) // 2 equal) are at most 8, and in every group one band holds exactly 8.
All inputs are finite; a program needn't handle non-finite values.
Results may differ from a plain program's by a relative error of at most 0.019.
Values may be sent and summed in bfloat16 or wider, within the bound.
A program may use at most 192 MiB of HBM per device.

v0:
```python
import math

import jax
import jax.numpy as jnp
from jax import lax
from jax.sharding import PartitionSpec as P

RADIX = 32
TS = 64


Z_BOTTOM = -2.0
Z_TOP = 2.0
DECAY_RATE = 0.5
COURANT = 0.3


def for_sending(shard):

    def short(part):
        return part.astype(jnp.bfloat16) if part.dtype == jnp.float32 else part

    return jax.tree.map(short, shard)


def refine(field):
    return jnp.repeat(jnp.repeat(field, 2, axis=0), 2, axis=1)


def upwind_flux(values, speeds, axis):
    widths = tuple(((1, 1) if dim_index == axis else (0, 0) for dim_index in range(3)))
    padded = jnp.pad(values, widths, mode="edge")
    speed_pad = jnp.pad(speeds, widths, mode="edge")
    count_faces = padded.shape[axis] - 1
    left_vals = lax.slice_in_dim(padded, 0, count_faces, axis=axis)
    right_vals = lax.slice_in_dim(padded, 1, count_faces + 1, axis=axis)
    face_speed = 0.5 * (
        lax.slice_in_dim(speed_pad, 0, count_faces, axis=axis)
        + lax.slice_in_dim(speed_pad, 1, count_faces + 1, axis=axis)
    )
    face_flux = jnp.maximum(face_speed, 0.0) * left_vals + jnp.minimum(face_speed, 0.0) * right_vals
    return lax.slice_in_dim(face_flux, 1, count_faces, axis=axis) - lax.slice_in_dim(
        face_flux, 0, count_faces - 1, axis=axis
    )


def patch_step(state, height, along_x, along_y):
    levels = state.shape[0]
    side = state.shape[1]
    spacing = (Z_TOP - Z_BOTTOM) / levels
    level_z = (Z_BOTTOM + (jnp.arange(levels, dtype=jnp.float32) + 0.5) * spacing)[:, None, None]
    fine_h = refine(height)[None]
    from_sea = jnp.clip((fine_h - level_z) / spacing + 0.5, 0.0, 1.0)
    position = jnp.arange(side, dtype=jnp.float32)
    edge_dist = jnp.minimum(position, side - 1.0 - position)
    distance = jnp.minimum(edge_dist[:, None], edge_dist[None, :])
    weight = 0.3 + 0.7 * jnp.exp(-8.0 * distance / side)
    blended = weight * from_sea + (1.0 - weight) * state.astype(jnp.float32)
    profile = jnp.exp(DECAY_RATE * (level_z - Z_TOP))
    speed_x = refine(along_x)[None] * profile
    speed_y = refine(along_y)[None] * profile
    moved = blended - COURANT * (
        upwind_flux(blended, speed_x, 2) + upwind_flux(blended, speed_y, 1)
    )
    updated = jnp.clip(moved, 0.0, 1.0)
    column = Z_BOTTOM + spacing * jnp.sum(updated, axis=0)
    coarse = column.reshape(side // 2, 2, side // 2, 2).mean(axis=(1, 3))
    return (updated.astype(jnp.bfloat16), coarse)


def small_tables(length):
    index_row = jnp.arange(length, dtype=jnp.int32)
    phase = index_row[:, None] * index_row[None, :] % length
    angle = phase.astype(jnp.float32) * (2.0 * math.pi / length)
    return (jnp.cos(angle).astype(jnp.bfloat16), jnp.sin(angle).astype(jnp.bfloat16))


def contract(data, table, pattern):
    return jnp.einsum(pattern, data, table, preferred_element_type=jnp.float32)


def factored_transform(real_in, imag_in, direction_sign, real_only):
    length = real_in.shape[-1]
    leading = real_in.shape[:-1]
    inner_size = length // RADIX
    cos_p, sin_p = small_tables(RADIX)
    cos_q, sin_q = small_tables(inner_size)
    split_re = real_in.reshape(leading + (RADIX, inner_size))
    segment_re = contract(split_re, cos_p, "...pq,pk->...kq")
    segment_im = direction_sign * contract(split_re, sin_p, "...pq,pk->...kq")
    if imag_in is not None:
        split_im = imag_in.reshape(leading + (RADIX, inner_size))
        segment_re = segment_re - direction_sign * contract(split_im, sin_p, "...pq,pk->...kq")
        segment_im = segment_im + contract(split_im, cos_p, "...pq,pk->...kq")
    first_idx = jnp.arange(RADIX, dtype=jnp.int32)[:, None]
    second_idx = jnp.arange(inner_size, dtype=jnp.int32)[None, :]
    angle = (first_idx * second_idx % length).astype(jnp.float32) * (2.0 * math.pi / length)
    twist_cos = jnp.cos(angle)
    twist_sin = jnp.sin(angle)
    turned_re = (segment_re * twist_cos - direction_sign * segment_im * twist_sin).astype(
        jnp.bfloat16
    )
    turned_im = (segment_im * twist_cos + direction_sign * segment_re * twist_sin).astype(
        jnp.bfloat16
    )
    out_re = contract(turned_re, cos_q, "...kq,qm->...km") - direction_sign * contract(
        turned_im, sin_q, "...kq,qm->...km"
    )
    out_re = jnp.swapaxes(out_re, -1, -2).reshape(leading + (length,))
    if real_only:
        return out_re
    out_im = contract(turned_im, cos_q, "...kq,qm->...km") + direction_sign * contract(
        turned_re, sin_q, "...kq,qm->...km"
    )
    out_im = jnp.swapaxes(out_im, -1, -2).reshape(leading + (length,))
    return (out_re, out_im)


def signed_waves(index_values, length):
    signed = (index_values + length // 2) % length - length // 2
    return signed.astype(jnp.float32) * (2.0 * math.pi / length)


def shards(eta_hat, phi_hat, patch_tiles, fraction):
    row_count = eta_hat.shape[1]
    length = eta_hat.shape[2]
    n_wide = lax.axis_size("wide")
    me_wide = lax.axis_index("wide")
    me_grp = lax.axis_index("grp")
    me_flat = lax.axis_index(("wide", "grp"))
    wave_cols = signed_waves(jnp.arange(length, dtype=jnp.int32), length)
    wave_rows = signed_waves(me_flat * row_count + jnp.arange(row_count, dtype=jnp.int32), length)
    phi_re = phi_hat[0].astype(jnp.float32)
    phi_im = phi_hat[1].astype(jnp.float32)
    real_in = jnp.stack(
        [
            eta_hat[0],
            (-wave_rows[:, None] * phi_im).astype(jnp.bfloat16),
            (-wave_cols[None, :] * phi_im).astype(jnp.bfloat16),
        ]
    )
    imag_in = jnp.stack(
        [
            eta_hat[1],
            (wave_rows[:, None] * phi_re).astype(jnp.bfloat16),
            (wave_cols[None, :] * phi_re).astype(jnp.bfloat16),
        ]
    )
    half_re, half_im = factored_transform(real_in, imag_in, 1.0, False)
    inverse_rows = jnp.swapaxes(
        jnp.concatenate([half_re.astype(jnp.bfloat16), half_im.astype(jnp.bfloat16)]), 1, 2
    )
    turned = lax.all_to_all(inverse_rows, ("wide", "grp"), split_axis=1, concat_axis=2, tiled=True)
    physical = factored_transform(turned[0:3], turned[3:6], 1.0, True)
    band_fields = lax.all_to_all(
        physical.astype(jnp.bfloat16), "grp", split_axis=2, concat_axis=1, tiled=True
    ).astype(physical.dtype)
    band_rows = band_fields.shape[1]
    band_cols = band_fields.shape[2]
    tile_rows = band_rows // TS
    tile_cols = band_cols // TS
    tiles_side = length // TS
    per_group = 2 * n_wide
    group_list = lax.dynamic_slice_in_dim(patch_tiles, me_grp * per_group, per_group)
    row_of = group_list // tiles_side
    col_of = group_list % tiles_side - me_grp * tile_cols
    my_ranks = jnp.arange(2, dtype=jnp.int32) * n_wide + me_wide
    local_t = jnp.arange(tile_rows * tile_cols, dtype=jnp.int32)
    tile_id = (
        (me_wide * tile_rows + local_t // tile_cols) * tiles_side
        + me_grp * tile_cols
        + local_t % tile_cols
    )
    matches = tile_id[:, None] == group_list[None, :]
    active = jnp.any(matches, axis=1)
    rank_index = jnp.sum(
        jnp.where(matches, jnp.arange(per_group, dtype=jnp.int32)[None, :], 0), axis=1
    )
    column_strip = lax.all_gather(
        band_fields.astype(jnp.bfloat16), "wide", axis=1, tiled=True
    ).astype(band_fields.dtype)

    def pick_strip(rank):
        return lax.dynamic_slice(
            column_strip, (0, row_of[rank] * TS, col_of[rank] * TS), (3, TS, TS)
        )

    footprints = jax.vmap(pick_strip)(my_ranks)
    new_states, coarse = jax.vmap(patch_step)(
        fraction[:, 0], footprints[:, 0], footprints[:, 1], footprints[:, 2]
    )
    coarse_flat = coarse.reshape(2, TS * TS)
    every_result = (
        lax.all_gather(
            coarse_flat.reshape(2, 1, TS * TS).astype(jnp.bfloat16), "wide", axis=1, tiled=True
        )
        .astype(jnp.float32)
        .reshape(per_group, TS * TS)
    )
    picked = every_result[rank_index]
    band_tiles = (
        band_fields[0]
        .reshape(tile_rows, TS, tile_cols, TS)
        .transpose(0, 2, 1, 3)
        .reshape(tile_rows * tile_cols, TS * TS)
    )
    corrected = jnp.where(active[:, None], picked, band_tiles)
    surface_band = (
        corrected.reshape(tile_rows, tile_cols, TS, TS)
        .transpose(0, 2, 1, 3)
        .reshape(band_rows, band_cols)
    )
    surface = lax.all_to_all(
        for_sending(surface_band), "grp", split_axis=0, concat_axis=1, tiled=True
    ).astype(surface_band.dtype)
    along_x = physical[1]
    along_y = physical[2]
    drive = (-(surface + 0.5 * (along_x * along_x + along_y * along_y))).astype(jnp.bfloat16)
    drive_re, drive_im = factored_transform(drive, None, -1.0, False)
    pair_rows = jnp.swapaxes(
        jnp.stack([drive_re.astype(jnp.bfloat16), drive_im.astype(jnp.bfloat16)]), 1, 2
    )
    pair_cols = lax.all_to_all(pair_rows, ("wide", "grp"), split_axis=1, concat_axis=2, tiled=True)
    spec_re, spec_im = factored_transform(pair_cols[0], pair_cols[1], -1.0, False)
    tendency = jnp.stack([spec_re, spec_im]) * (1.0 / length)
    return (surface, new_states[:, None], tendency)


def solution(mesh):
    placed = (
        P(None, ("wide", "grp"), None),
        P(None, ("wide", "grp"), None),
        P(),
        P(None, ("wide", "grp"), None, None, None),
    )
    return jax.shard_map(
        shards,
        mesh=mesh,
        in_specs=placed,
        out_specs=(
            P(("wide", "grp"), None),
            P(None, ("wide", "grp"), None, None, None),
            P(None, ("wide", "grp"), None),
        ),
        check_vma=False,
    )
```

profile of v0, /device:TPU:1, one launch (start us, length us, event | category | flops | bytes accessed | tf_op | source)
XLA Modules:
  0.0 338.9 jit_solution(14497222716978649175)
XLA Ops:
  7.4 0.9 fusion.251
  8.4 1.0 fusion.42
  13.8 0.8 convert_element_type.411
  15.0 0.8 convert_element_type.408
  15.9 4.1 %copy.124 = bf16[6,2048,16]{2,0,1:T(8,128)(2,1)} copy(bf16[6,2048,16]{1,2,0:T(8,128)(2,1)S(1)} %maximum_bitcast_fusion) | data formatting | bytes 786432 | tf_op jit(solution)/shard_map/transpose | solution.py:150
  20.0 5.6 %reshape.527 = bf16[128,2,768]{2,1,0:T(2,128)(2,1)S(1)} reshape(bf16[2048,6,16]{2,1,0:T(8,128)(2,1)} %bitcast.240) | data formatting | bytes 786432
  25.6 24.1 %all_to_all.58 = bf16[128,2,768]{2,1,0:T(2,128)(2,1)S(1)} all-to-all(bf16[128,2,768]{2,1,0:T(2,128)(2,1)S(1)} %reshape.527), channel_id=1, replica_groups=mesh['wide'=16,'grp'=8] {'wide','grp'}, dimensions={0} | all-to-all | bytes 786432 | tf_op jit(solution)/shard_map/all_to_all | solution.py:153
  49.7 4.8 %reshape.528 = bf16[2048,6,16]{2,1,0:T(8,128)(2,1)} reshape(bf16[128,2,768]{2,1,0:T(2,128)(2,1)S(1)} %all_to_all.58) | data formatting | bytes 786432
  54.6 6.1 %copy.158 = bf16[6,128,16,16]{2,1,3,0:T(8,128)(2,1)S(1)} copy(bf16[6,128,16,16]{3,0,2,1:T(8,128)(2,1)} %bitcast.239) | data formatting | bytes 786432 | tf_op jit(solution)/shard_map/all_to_all | solution.py:153
  60.7 1.9 fusion.249
  62.6 4.3 %copy.126 = bf16[3,16,128,16]{3,2,1,0:T(8,128)(2,1)S(1)} copy(bf16[3,16,128,16]{1,2,3,0:T(8,128)(2,1)} %get-tuple-element.58) | data formatting | bytes 393216 | tf_op jit(solution)/shard_map/slice | solution.py:154
  67.7 1.2 fusion.99
  69.0 1.3 fusion.106
  70.2 3.1 copy.127
  74.2 1.5 convolution_add_fusion
  75.6 1.5 convolution_subtract_fusion.1
  77.9 3.4 %copy.159 = bf16[3,16,64,32]{1,0,3,2:T(4,128)(2,1)S(1)} copy(bf16[3,16,64,32]{2,3,1,0:T(8,128)(2,1)S(1)} %get-tuple-element.82) | data formatting | bytes 393216 | tf_op jit(solution)/shard_map/convert_element_type | solution.py:156
  81.3 1.9 reshape.529
  83.2 9.3 %all_to_all.59 = bf16[8,2,6144]{2,1,0:T(2,128)(2,1)S(1)} all-to-all(bf16[8,2,6144]{2,1,0:T(2,128)(2,1)S(1)} %reshape.529), channel_id=1, replica_groups=mesh['wide'=16,'grp'=8] {'grp'}, dimensions={0} | all-to-all | bytes 393216 | tf_op jit(solution)/shard_map/all_to_all | solution.py:155
  92.5 2.0 reshape.530
  94.5 2.0 copy.161
  99.9 1.0 copy.160
  101.1 39.6 %all-gather.2.cloned.1.call-done = bf16[3,2048,256]{2,1,0:T(8,128)(2,1)} async-done(((bf16[3,128,256]{2,1,0:T(8,128)(2,1)}), bf16[3,2048,256]{2,1,0:T(8,128)(2,1)}) %all-gather.2.cloned.1.call-update) | async-done | bytes 3145744 | tf_op jit(solution)/shard_map/all_gather | solution.py:179
  140.7 5.1 %convert_element_type.418 = f32[3,2048,256]{2,1,0:T(8,128)} convert(bf16[3,2048,256]{2,1,0:T(8,128)(2,1)} %all-gather.2.cloned.1.call-done) | non-fusion elementwise | flops 1572864 | bytes 9437184 | tf_op jit(solution)/shard_map/convert_element_type | solution.py:181
  145.8 5.9 %while.1 = (s32[]{:T(128)}, f32[3,2048,256]{2,1,0:T(8,128)}, s32[2,3]{1,0:T(2,128)S(1)}, f32[2,3,64,64]{3,2,1,0:T(8,128)S(1)}, s32[]{:T(128)}) while((s32[]{:T(128)}, f32[3,2048,256]{2,1,0:T(8,128)}, s32[2,3]{1,0:T(2,128)S(1)}, f32[2,3,64,64]{3,2,1,0:T(8,128)S(1)}, s32[]{:T(128)}) %tuple.55), condition=%wide.while_cond, body=%wide.while_body.sunk | while | flops 2 | bytes 147581 | solution.py:184
  146.4 2.3 bitcast_dynamic-update-slice_fusion.2
  149.3 2.3 bitcast_dynamic-update-slice_fusion.2
  152.3 0.9 slice_bitcast_fusion.1
  153.5 3.9 %fusion.8 = f32[2,64,128,128]{3,2,1,0:T(8,128)S(1)} fusion(bf16[2,1,64,128,128]{4,3,2,1,0:T(8,128)(2,1)} %param.7, f32[128,128]{1,0:T(8,128)S(1)} %get-tuple-element.81, f32[64]{0:T(128)S(1)} %fusion.129, f32[2,128,128]{2,1,0:T(8,128)S(1)} %copy.134, f32[128,128]{1,0:T(8,128)S(1)} %get-tuple-element.80), kind=kLoop, calls=%fused_computation.22 | loop fusion | flops 16777216 | bytes 12845312 | tf_op jit(solution)/shard_map/vmap()/add | solution.py:58
  157.6 7.7 %fusion.246 = (f32[2,64,128,1]{3,2,1,0:T(8,128)}, f32[2,64,128,1]{3,2,1,0:T(8,128)}) fusion(f32[2,64,128,128]{3,2,1,0:T(8,128)S(1)} %fusion.8), kind=kLoop, calls=%fused_computation.353 | loop fusion | bytes 262144 | tf_op jit(solution)/shard_map/vmap(jit(_pad))/slice | solution.py:32
  166.4 5.4 %broadcast_multiply_fusion.1 = (f32[2,64,128,128]{3,2,1,0:T(8,128)}, f32[2,64,128,128]{3,2,1,0:T(8,128)S(1)}) fusion(f32[64]{0:T(128)S(1)} %multiply_exponential_fusion, f32[2,128,128]{2,1,0:T(8,128)S(1)} %copy.137, f32[2,128,128]{2,1,0:T(8,128)S(1)} %copy.139), kind=kLoop, calls=%fused_computation.25 | loop fusion | flops 4194304 | bytes 17039616 | tf_op jit(solution)/shard_map/vmap()/mul | solution.py:60
  171.8 3.2 copy-done.1
  175.2 13.3 %fusion.245 = (f32[2,64,128,1]{3,2,1,0:T(8,128)}, f32[2,64,128,1]{3,2,1,0:T(8,128)}) fusion(f32[2,64,128,128]{3,2,1,0:T(8,128)} %get-tuple-element.78), kind=kLoop, calls=%fused_computation.352 | loop fusion | bytes 262144 | tf_op jit(solution)/shard_map/vmap(jit(_pad))/slice | solution.py:33
  188.5 12.6 %fusion.3 = f32[2,64,129,128]{3,2,1,0:T(8,128)} fusion(f32[2,64,128,128]{3,2,1,0:T(8,128)S(1)} %bitcast.236, f32[2,64,1,128]{3,2,1,0:T(1,128)S(1)} %get-tuple-element.56, f32[2,64,1,128]{3,2,1,0:T(1,128)S(1)} %get-tuple-element.55, f32[2,64,1,128]{3,2,1,0:T(1,128)S(1)} %get-tuple-element.54, f32[2,64,128,128]{3,2,1,0:T(8,128)} %copy-done.1, ...), kind=kLoop, calls=%fused_computation.13 | loop fusion | flops 23248896 | bytes 25493504 | tf_op jit(solution)/shard_map/vmap()/add | solution.py:41
  201.1 25.7 %fusion.1 = f32[2,64,128,129]{3,2,1,0:T(8,128)} fusion(f32[2,64,128,128]{3,2,1,0:T(8,128)S(1)} %bitcast.236, f32[2,64,128,1]{3,2,1,0:T(8,128)} %get-tuple-element.52, f32[2,64,128,1]{3,2,1,0:T(8,128)} %get-tuple-element.51, f32[2,64,128,1]{3,2,1,0:T(8,128)} %get-tuple-element.50, f32[2,64,128,128]{3,2,1,0:T(8,128)} %get-tuple-element.78, ...), kind=kLoop, calls=%fused_computation.8 | loop fusion | flops 23248896 | bytes 25493504 | tf_op jit(solution)/shard_map/vmap()/add | solution.py:41
  226.8 22.0 %convert_bitcast_fusion = (bf16[2,1,64,128,128]{4,3,2,1,0:T(8,128)(2,1)}, f32[2,64,128,128]{3,2,1,0:T(8,128)}) fusion(f32[2,64,129,128]{3,2,1,0:T(8,128)} %fusion.3, f32[2,64,128,129]{3,2,1,0:T(8,128)} %fusion.1, bf16[2,1,64,128,128]{4,3,2,1,0:T(8,128)(2,1)} %param.7, f32[128,128]{1,0:T(8,128)S(1)} %get-tuple-element.81, f32[64]{0:T(128)S(1)} %fusion.129, ...), kind=kLoop, calls=%fused_computation.23 | loop fusion | flops 31457280 | bytes 50594048 | tf_op jit(solution)/shard_map/broadcast_in_dim | solution.py:226
  248.8 3.8 %reduce_sum.29 = f32[2,128,128]{2,1,0:T(8,128)S(1)} reduce(f32[2,64,128,128]{3,2,1,0:T(8,128)} %get-tuple-element.44, f32[]{:T(128)} %constant.200.clone.1), dimensions={1}, to_apply=%region_1.2 | reduce | flops 2064384 | bytes 8519684 | tf_op jit(solution)/shard_map/vmap()/reduce_sum | solution.py:66
  252.7 9.8 %add.508 = f32[2,64,2,64,2]{4,3,2,1,0:T(8,128)} reshape(f32[2,128,128]{2,1,0:T(8,128)S(1)} %multiply_add_fusion) | data formatting | bytes 262144 | tf_op jit(solution)/shard_map/vmap()/add | solution.py:66
  262.4 4.5 %reduce_sum.30 = f32[2,64,64]{2,1,0:T(8,128)S(1)} reduce(f32[2,64,2,64,2]{4,3,2,1,0:T(8,128)} %add.508, f32[]{:T(128)} %constant.200.clone.1), dimensions={2,4}, to_apply=%region_2.3 | reduce | flops 24576 | bytes 163844 | tf_op jit(solution)/shard_map/vmap()/reduce_sum | solution.py:67
  267.1 17.1 %all_gather.7 = bf16[2,16,4096]{2,0,1:T(2,128)(2,1)S(1)} all-gather(bf16[2,1,4096]{2,0,1:T(2,128)(2,1)S(1)} %convert_element_type.422), channel_id=1, replica_groups=mesh['wide'=16,'grp'=8] {'wide'}, dimensions={1}, use_global_device_ids=true | all-gather | bytes 278528 | tf_op jit(solution)/shard_map/all_gather | solution.py:194
  286.1 11.1 %all-to-all-start.2 = ((bf16[8,16,256]{2,1,0:T(8,128)(2,1)}), bf16[8,16,256]{2,1,0:T(8,128)(2,1)S(1)}, u32[]{:S(2)}, u32[]{:S(2)}) async-start(bf16[8,16,256]{2,1,0:T(8,128)(2,1)} %convert_element_type.425), calls=%async_computation.2 | async-start | bytes 131072 | tf_op jit(solution)/shard_map/all_to_all | solution.py:213
  297.6 4.4 %all-to-all-done.2 = bf16[8,16,256]{2,1,0:T(8,128)(2,1)S(1)} async-done(((bf16[8,16,256]{2,1,0:T(8,128)(2,1)}), bf16[8,16,256]{2,1,0:T(8,128)(2,1)S(1)}, u32[]{:S(2)}, u32[]{:S(2)}) %all-to-all-start.2) | async-done | bytes 65568 | tf_op jit(solution)/shard_map/all_to_all | solution.py:213
  305.7 1.5 reshape.531
  307.2 4.9 %all-to-all-start.3 = ((bf16[128,2,256]{2,1,0:T(2,128)(2,1)}), bf16[128,2,256]{2,1,0:T(2,128)(2,1)S(1)}, u32[]{:S(2)}, u32[]{:S(2)}) async-start(bf16[128,2,256]{2,1,0:T(2,128)(2,1)} %reshape.531), calls=%async_computation.3 | async-start | bytes 262144 | tf_op jit(solution)/shard_map/all_to_all | solution.py:223
  312.8 9.3 %all-to-all-done.3 = bf16[128,2,256]{2,1,0:T(2,128)(2,1)S(1)} async-done(((bf16[128,2,256]{2,1,0:T(2,128)(2,1)}), bf16[128,2,256]{2,1,0:T(2,128)(2,1)S(1)}, u32[]{:S(2)}, u32[]{:S(2)}) %all-to-all-start.3) | async-done | bytes 131104 | tf_op jit(solution)/shard_map/all_to_all | solution.py:223
  322.8 2.0 copy.162
  324.9 1.1 copy.150
  326.8 1.1 copy.151
  (142 shorter events, 26.0 us)
Async XLA Ops:
  7.2 133.5 %all-gather.2.cloned.1.call-start = ((), (), s32[]{:S(2)}) async-start(), calls=%async_computation.4 | async-start | bytes 3342336 | tf_op jit(solution)/shard_map/all_gather | solution.py:179
  7.3 6.5 %copy-start.3 = (f32[32,64]{1,0:T(8,128)}, f32[32,64]{1,0:T(8,128)S(1)}, u32[]{:S(2)}) copy-start(f32[32,64]{1,0:T(8,128)S(1)} %get-tuple-element.88) | copy-start | bytes 24580
  62.6 7.6 %copy-start.2 = (bf16[3,16,128,16]{1,2,3,0:T(8,128)(2,1)S(1)}, bf16[3,16,128,16]{1,2,3,0:T(8,128)(2,1)}, u32[]{:S(2)}) copy-start(bf16[3,16,128,16]{1,2,3,0:T(8,128)(2,1)} %get-tuple-element.57) | copy-start | bytes 589828
  70.2 6.9 %copy-start.4 = (f32[32,64]{1,0:T(8,128)S(1)}, f32[32,64]{1,0:T(8,128)}, u32[]{:S(2)}) copy-start(f32[32,64]{1,0:T(8,128)} %copy-done.3) | copy-start | bytes 24580
  77.1 19.5 %copy-start.8 = (s32[256]{0:T(256)S(1)}, s32[256]{0:T(256)}, u32[]{:S(2)}) copy-start(s32[256]{0:T(256)} %param.6) | copy-start | bytes 3076
  151.6 0.7 copy-start.5
  157.5 8.4 %copy-start = (f32[2,64,128,128]{3,2,1,0:T(8,128)}, f32[2,64,128,128]{3,2,1,0:T(8,128)S(1)}, u32[]{:S(2)}) copy-start(f32[2,64,128,128]{3,2,1,0:T(8,128)S(1)} %fusion.8) | copy-start | bytes 25165828
  166.4 22.1 %slice-start = ((s8[8388608]{0:T(1024)(128)(4,1)}), s8[4194304]{0:T(1024)(128)(4,1)S(1)}, s32[]{:S(2)}) async-start(s8[8388608]{0:T(1024)(128)(4,1)} %bitcast.235), calls=%async_computation.5 | async-start | bytes 8388608
  171.8 3.2 copy-start.1
  175.2 13.3 %slice-start.1 = ((s8[8388608]{0:T(1024)(128)(4,1)}), s8[4194304]{0:T(1024)(128)(4,1)S(1)}, s32[]{:S(2)}) async-start(s8[8388608]{0:T(1024)(128)(4,1)} %bitcast.235), calls=%async_computation.6 | async-start | bytes 8388608
  252.6 32.5 %copy-start.7 = (pred[2,4]{1,0:T(4,128)(4,1)S(1)}, pred[2,4]{1,0:T(4,128)(4,1)}, u32[]{:S(2)}) copy-start(pred[2,4]{1,0:T(4,128)(4,1)} %broadcast_in_dim.29) | copy-start | bytes 28
  262.4 40.0 %copy-start.6 = (f32[32,64]{1,0:T(8,128)S(1)}, f32[32,64]{1,0:T(8,128)}, u32[]{:S(2)}) copy-start(f32[32,64]{1,0:T(8,128)} %get-tuple-element.93) | copy-start | bytes 24580
  286.1 15.9 %all-to-all-start.2 = ((bf16[8,16,256]{2,1,0:T(8,128)(2,1)}), bf16[8,16,256]{2,1,0:T(8,128)(2,1)S(1)}, u32[]{:S(2)}, u32[]{:S(2)}) async-start(bf16[8,16,256]{2,1,0:T(8,128)(2,1)} %convert_element_type.425), calls=%async_computation.2 | async-start | bytes 131072 | tf_op jit(solution)/shard_map/all_to_all | solution.py:213
  307.2 14.9 %all-to-all-start.3 = ((bf16[128,2,256]{2,1,0:T(2,128)(2,1)}), bf16[128,2,256]{2,1,0:T(2,128)(2,1)S(1)}, u32[]{:S(2)}, u32[]{:S(2)}) async-start(bf16[128,2,256]{2,1,0:T(2,128)(2,1)} %reshape.531), calls=%async_computation.3 | async-start | bytes 262144 | tf_op jit(solution)/shard_map/all_to_all | solution.py:223
Sparse Core Ops, SparseCore 0:
  96.7 44.0 all-gather.1
where the time goes:
time: 346 us; the launch traced here: 339 us
  local copies, waits for them, and re-layouts  104 us (30%)
  other arithmetic  86.5 us (25%)
  waiting for transfers between devices  53.3 us (15%)
  blocking collectives  50.5 us (15%)
  starting transfers between devices  16 us (5%)
  between operations  15.4 us (4%)
  matrix products  13 us (4%)
    all_gather x1, waiting for transfers between devices, shards(): lax.all_gather(band_fields.astype(jnp.bfloat16), 'wide', axis=1, tiled=True)  39.6 us
    add x2, other arithmetic, upwind_flux(): jnp.maximum(face_speed, 0.0) * left_vals  38.3 us
    all_to_all x1, blocking collectives, shards(): lax.all_to_all(inverse_rows, ('wide', 'grp'), split_axis=1, concat_axis=2...  24.1 us
    broadcast_in_dim x1, other arithmetic, shards(): return (surface, new_states[:, None], tendency)  22 us
    unnamed x33, local copies, waits for them, and re-layouts  21.2 us
    all_gather x1, blocking collectives, shards(): lax.all_gather(coarse_flat.reshape(2, 1, TS * TS).astype(jnp.bfloat16), '...  17.1 us
    slice x2, local copies, waits for them, and re-layouts, upwind_flux(): speed_pad = jnp.pad(speeds, widths, mode='edge')  13.4 us
    dot_general x28, matrix products, contract(): return jnp.einsum(pattern, data, table, preferred_element_type=jnp.float32)  13 us
  transfers between devices with their start and end apart: 3, of which 3 were waited for; matrix products, arithmetic and copies ran while one was open for 2% of the time, Pallas kernels for 0%

commit v1 on v0

v1 whole, which is shorter than its diff:
```python
import functools
import math

import jax
import jax.numpy as jnp
import numpy as np
from jax import lax
from jax.experimental import pallas as pl
from jax.experimental.pallas import tpu as pltpu
from jax.sharding import PartitionSpec as P

F32 = jnp.float32
BF16 = jnp.bfloat16
MESH = pl.DeviceIdType.MESH

N = 2048
D = 128
NW = 16
NG = 8
L = 128
R = 16
LV = 64
SIDE = 128
TS = 64
Z_BOTTOM = -2.0
Z_TOP = 2.0
DECAY_RATE = 0.5
COURANT = 0.3
VMEM_LIMIT = 56 << 20


def unit(phase, length):
    angle = (phase % length) * (2.0 * math.pi / length)
    return np.cos(angle), np.sin(angle)


def lane_tables(sign):
    k1 = np.arange(R)[:, None]
    n2 = np.arange(L)[None, :]
    tc, ts = unit(k1 * n2, N)
    k2 = np.arange(D)[:, None]
    c, s = unit(k2 * n2, D)
    spread = np.concatenate([c, sign * s], axis=1)
    return (
        jnp.asarray(tc, F32),
        jnp.asarray(sign * ts, F32),
        jnp.asarray(spread, F32).astype(BF16),
    )


def block_tables(sign, blocks, full):
    k1 = np.arange(D)[:, None]
    src = np.arange(D)[None, :]
    c, s = unit(k1 * src, D)
    gather = np.concatenate([c, sign * s], axis=0)
    j = np.tile(np.arange(R), 8)[None, :]
    tc, ts = unit(k1 * j, N)
    k2 = np.arange(R)[:, None]
    jj = np.arange(R)[None, :]
    cc, ss = unit(k2 * jj, R)
    ss = sign * ss
    rows = []
    for part in range(2 if full else 1):
        for e in range(blocks):
            out = np.zeros((R, 2, 4, R))
            out[:, 0, e, :] = cc if part == 0 else ss
            out[:, 1, e, :] = -ss if part == 0 else cc
            rows.append(out.reshape(R, L))
    finish = np.concatenate(rows, axis=0)
    return (
        jnp.asarray(gather, F32).astype(BF16),
        jnp.asarray(tc, F32),
        jnp.asarray(sign * ts, F32),
        jnp.asarray(finish, F32).astype(BF16),
    )


def fourth(x, sign):
    (ar, ai), (br, bi), (cr, ci), (dr, di) = x
    t0r, t0i, t1r, t1i = ar + cr, ai + ci, ar - cr, ai - ci
    t2r, t2i, t3r, t3i = br + dr, bi + di, br - dr, bi - di
    if sign < 0:
        t3r, t3i = -t3r, -t3i
    return (
        (t0r + t2r, t0i + t2i),
        (t1r - t3i, t1i + t3r),
        (t0r - t2r, t0i - t2i),
        (t1r + t3i, t1i - t3r),
    )


def times(x, re, im):
    if abs(im) < 1e-12 and abs(re - 1.0) < 1e-12:
        return x
    a, b = x
    return (a * re - b * im, a * im + b * re)


def sixteenth(x, sign):
    inner = []
    for b in range(4):
        y = fourth([x[4 * a + b] for a in range(4)], sign)
        turned = []
        for c in range(4):
            angle = sign * 2.0 * math.pi * b * c / 16
            turned.append(times(y[c], math.cos(angle), math.sin(angle)))
        inner.append(turned)
    out = [None] * 16
    for c in range(4):
        z = fourth([inner[b][c] for b in range(4)], sign)
        for d in range(4):
            out[c + 4 * d] = z[d]
    return out


def nt_dot(a, b):
    return lax.dot_general(a, b, (((1,), (1,)), ((), ())), preferred_element_type=F32)


def blocks_in(x, gather, tc, ts, flip):
    both = jnp.dot(gather, x, preferred_element_type=F32)
    parts = []
    for h in range(2):
        a = both[:D, h * L:(h + 1) * L]
        b = both[D:, h * L:(h + 1) * L]
        u = a * tc - b * ts
        v = b * tc + a * ts
        parts.append((u + flip * pltpu.roll(v, 64, 1)).astype(BF16))
    return jnp.concatenate(parts, axis=0)


def coords(flat):
    return (flat // NG, flat % NG)


def lane_iota(rows):
    return lax.broadcasted_iota(jnp.int32, (rows, L), 1)


def greet_all(me):
    barrier = pltpu.get_barrier_semaphore()

    def greet(k, carry):
        pl.semaphore_signal(
            barrier, inc=1, device_id=coords(lax.rem(me + k, D)), device_id_type=MESH
        )
        return carry

    lax.fori_loop(1, D, greet, 0)
    return barrier


def rise_kernel(
    tiles, eta, phi, tw_c, tw_s, spread, gather, bt_c, bt_s, finish,
    phys, foot,
    tb, wide32, send, recv, send1, recv1, send2, recv2,
    ssem, rsem, ssem1, rsem1, ssem2, rsem2,
):
    w = lax.axis_index("wide")
    g = lax.axis_index("grp")
    me = w * NG + g
    barrier = greet_all(me)

    row = lax.broadcasted_iota(jnp.int32, (R, L), 0)
    lane = lane_iota(R)
    kx = me * R + row
    kx = jnp.where(kx >= N // 2, kx - N, kx).astype(F32) * (2.0 * math.pi / N)

    for f in range(3):
        x = []
        for n1 in range(16):
            cols = slice(n1 * L, (n1 + 1) * L)
            if f == 0:
                x.append((eta[0, :, cols].astype(F32), eta[1, :, cols].astype(F32)))
            else:
                if f == 1:
                    k = kx
                else:
                    base = n1 * L if n1 < 8 else n1 * L - N
                    k = (lane + base).astype(F32) * (2.0 * math.pi / N)
                x.append((-k * phi[1, :, cols].astype(F32), k * phi[0, :, cols].astype(F32)))
        y = sixteenth(x, 1)
        for k1 in range(16):
            c, s = tw_c[k1:k1 + 1, :], tw_s[k1:k1 + 1, :]
            a, b = y[k1]
            re = (a * c - b * s).astype(BF16)
            im = (a * s + b * c).astype(BF16)
            up = slice(f * R, (f + 1) * R)
            dn = slice(64 + f * R, 64 + (f + 1) * R)
            tb[k1, up, 0:L] = re
            tb[k1, up, L:2 * L] = -im
            tb[k1, dn, 0:L] = im
            tb[k1, dn, L:2 * L] = re

    zero = jnp.zeros((R, 2 * L), BF16)

    def rows_out(kk, carry):
        for h in range(2):
            tb[2 * kk + h, 48:64, :] = zero
            tb[2 * kk + h, 112:128, :] = zero
        rhs = tb[pl.ds(2 * kk, 2)].reshape(2 * L, 2 * L)
        z = nt_dot(spread[...], rhs)
        wide32[pl.ds(2 * kk, D, stride=R), :] = z[:, :L]
        wide32[pl.ds(2 * kk + 1, D, stride=R), :] = z[:, L:]
        return carry

    lax.fori_loop(0, 8, rows_out, 0)

    def narrow(i, carry):
        part = wide32[pl.ds(pl.multiple_of(i * 128, 128), 128), :]
        send[pl.ds(i * 8, 8)] = part.reshape(8, R, L).astype(BF16)
        return carry

    lax.fori_loop(0, 16, narrow, 0)

    pl.semaphore_wait(barrier, D - 1)
    pltpu.make_async_copy(send.at[me], recv.at[me], rsem).start()

    def post(k, carry):
        d = lax.rem(me + k, D)
        pltpu.make_async_remote_copy(
            send.at[d], recv.at[me], ssem, rsem, device_id=coords(d), device_id_type=MESH
        ).start()
        return carry

    lax.fori_loop(1, D, post, 0)
    pltpu.make_async_copy(recv, recv, rsem).wait()

    def widen(i, carry):
        part = recv[pl.ds(i * 8, 8)].astype(F32)
        wide32[pl.ds(pl.multiple_of(i * 128, 128), 128), :] = part.reshape(128, L)
        return carry

    lax.fori_loop(0, 16, widen, 0)

    flip = jnp.where(lane_iota(D) < 64, -1.0, 1.0).astype(F32)

    def columns(yy, carry):
        x = jnp.concatenate(
            [
                wide32[pl.ds(2 * yy, D, stride=R), :].astype(BF16),
                wide32[pl.ds(2 * yy + 1, D, stride=R), :].astype(BF16),
            ],
            axis=1,
        )
        t = blocks_in(x, gather[...], bt_c[...], bt_s[...], flip)
        out = nt_dot(finish[...], t)
        phys[pl.ds(2 * yy, 48, stride=R), :] = out[:, :L]
        phys[pl.ds(2 * yy + 1, 48, stride=R), :] = out[:, L:]
        return carry

    lax.fori_loop(0, 8, columns, 0)

    low = lane < 64

    def by_group(q, carry):
        for h in range(2):
            at = [pl.multiple_of((f * 16 + 2 * q + h) * R, R) for f in range(3)]
            ht = phys[pl.ds(at[0], R), :]
            vx = phys[pl.ds(at[1], R), :]
            vy = phys[pl.ds(at[2], R), :]
            send1[q, h] = ht.astype(BF16)
            send1[q, 2 + 2 * h] = jnp.where(low, vx, pltpu.roll(vy, 64, 1)).astype(BF16)
            send1[q, 3 + 2 * h] = jnp.where(low, pltpu.roll(vx, 64, 1), vy).astype(BF16)
        return carry

    lax.fori_loop(0, NG, by_group, 0)

    pltpu.make_async_copy(send1.at[g], recv1.at[g], rsem1).start()
    for k in range(1, NG):
        d = lax.rem(g + k, NG)
        pltpu.make_async_remote_copy(
            send1.at[d], recv1.at[g], ssem1, rsem1, device_id=(w, d), device_id_type=MESH
        ).start()
    pltpu.make_async_copy(recv1, recv1, rsem1).wait()

    def choose(d, carry):
        t0 = tiles[g * 32 + d]
        t1 = tiles[g * 32 + 16 + d]
        t = jnp.where(lax.shift_right_logical(t0, 6) == w, t0, t1)
        upper = jnp.bitwise_and(lax.shift_right_logical(t, 5), 1) * 4
        col = jnp.bitwise_and(t, 3)
        odd = jnp.bitwise_and(t, 1)
        pair = lax.shift_right_logical(col, 1)
        right = (lane * 0 + odd) == 1
        for q in range(4):
            send2[d, q] = recv1[upper + q, 2 + col]
        for q in range(2):
            a = recv1[upper + 2 * q, pair].astype(F32)
            b = recv1[upper + 2 * q + 1, pair].astype(F32)
            lo = jnp.where(right, pltpu.roll(a, 64, 1), a)
            hi = jnp.where(right, b, pltpu.roll(b, 64, 1))
            send2[d, 4 + q] = jnp.where(low, lo, hi).astype(BF16)
        return carry

    lax.fori_loop(0, NW, choose, 0)

    pltpu.make_async_copy(send2.at[w], recv2.at[w], rsem2).start()
    for k in range(1, NW):
        d = lax.rem(w + k, NW)
        pltpu.make_async_remote_copy(
            send2.at[d], recv2.at[w], ssem2, rsem2, device_id=(d, g), device_id_type=MESH
        ).start()
    pltpu.make_async_copy(recv2, recv2, rsem2).wait()

    for s in range(2):
        t = tiles[g * 32 + s * 16 + w]
        band = jnp.bitwise_and(lax.shift_right_logical(t, 6), NW - 1)
        for q in range(6):
            foot[s, q] = recv2[band, q]

    pltpu.make_async_copy(send.at[pl.ds(0, D - 1)], send.at[pl.ds(0, D - 1)], ssem).wait()
    pltpu.make_async_copy(send1.at[pl.ds(0, NG - 1)], send1.at[pl.ds(0, NG - 1)], ssem1).wait()
    pltpu.make_async_copy(send2.at[pl.ds(0, NW - 1)], send2.at[pl.ds(0, NW - 1)], ssem2).wait()


def patch_tables():
    pos = np.arange(SIDE)
    edge = np.minimum(pos, SIDE - 1 - pos)
    dist = np.minimum(edge[:, None], edge[None, :])
    weight = 0.3 + 0.7 * np.exp(-8.0 * dist / SIDE)
    x = np.arange(SIDE)
    pick = np.zeros((2, L, SIDE))
    for h in range(2):
        pick[h, 64 * h + x // 2, x] = 1.0
    rows = np.zeros((SIDE, TS))
    rows[x, x // 2] = 1.0
    halves = np.zeros((2, SIDE, 32))
    for i in range(SIDE):
        r = i // 2
        blk, within = r // 16, r % 16
        halves[blk % 2, i, (blk // 2) * 16 + within] = 1.0
    z = Z_BOTTOM + (np.arange(LV) + 0.5) * ((Z_TOP - Z_BOTTOM) / LV)
    prof = np.exp(DECAY_RATE * (z - Z_TOP))
    return (
        jnp.asarray(prof, F32),
        jnp.asarray(weight, F32),
        jnp.asarray(pick, F32).astype(BF16),
        jnp.asarray(rows, F32).astype(BF16),
        jnp.asarray(halves, F32).astype(BF16),
        jnp.asarray(np.swapaxes(pick, 1, 2), F32),
        jnp.asarray(rows.T, F32),
    )


RB = 16
PAD = 8


def patch_kernel(
    prof, foot, state, weight, pick, rows, halves, down_l, down_r,
    state_out, coarse,
    hh, cf, bl, total, gathered,
):
    s = pl.program_id(0)

    vel = foot[0, 0:4].reshape(64, L)
    hgt = foot[0, 4:6].reshape(32, L)

    def up(m, sel, spread_rows):
        wide = jnp.dot(m, sel, preferred_element_type=F32).astype(BF16)
        return jnp.dot(spread_rows, wide, preferred_element_type=F32)

    height = up(hgt, pick[0], halves[0]) + up(hgt, pick[1], halves[1])
    ax = up(vel, pick[0], rows[...])
    ay = up(vel, pick[1], rows[...])
    scale = LV / (Z_TOP - Z_BOTTOM)
    hh[...] = height * scale - Z_BOTTOM * scale

    lane = lax.broadcasted_iota(jnp.int32, (SIDE, SIDE), 1)
    sub = lax.broadcasted_iota(jnp.int32, (SIDE, SIDE), 0)

    def faces(a, axis, index):
        after = jnp.where(index == SIDE - 1, a, pltpu.roll(a, SIDE - 1, axis))
        before = jnp.where(index == 0, a, pltpu.roll(a, 1, axis))
        return (0.5 * COURANT) * (a + after), (0.5 * COURANT) * (before + a)

    center = jnp.zeros((SIDE, SIDE), F32)
    for n, (a, axis, index) in enumerate(((ax, 1, lane), (ay, 0, sub))):
        upper, lower = faces(a, axis, index)
        center += jnp.maximum(upper, 0.0) - jnp.minimum(lower, 0.0)
        from_up = jnp.minimum(upper, 0.0)
        from_low = -jnp.maximum(lower, 0.0)
        last, first = index == SIDE - 1, index == 0
        center += jnp.where(last, from_up, 0.0) + jnp.where(first, from_low, 0.0)
        cf[1 + 2 * n] = jnp.where(last, 0.0, from_up)
        cf[2 + 2 * n] = jnp.where(first, 0.0, from_low)
    cf[0] = center

    edge = jnp.zeros((PAD, SIDE), F32)
    for b in range(SIDE // RB):
        rs = slice(b * RB, (b + 1) * RB)
        h = hh[rs, :]
        wt = weight[rs, :]
        keep = 1.0 - wt

        def blend(k, carry, b=b, rs=rs, h=h, wt=wt, keep=keep):
            sea = jnp.clip(h - k.astype(F32), 0.0, 1.0)
            bl[k, PAD + b * RB:PAD + (b + 1) * RB, :] = (
                wt * sea + keep * state[0, k, rs, :].astype(F32)
            )
            if b == 0:
                bl[k, 0:PAD, :] = edge
            if b == SIDE // RB - 1:
                bl[k, PAD + SIDE:, :] = edge
            return carry

        lax.fori_loop(0, LV, blend, 0, unroll=4)

    for b in range(SIDE // RB):
        rs = slice(b * RB, (b + 1) * RB)
        at = PAD + b * RB
        c0, c1, c2, c3, c4 = (cf[n, rs, :] for n in range(5))

        def move(k, acc, at=at, rs=rs, c0=c0, c1=c1, c2=c2, c3=c3, c4=c4):
            mid = bl[k, at:at + RB, :]
            nxt = bl[k, at + 1:at + 1 + RB, :]
            prv = bl[k, at - 1:at - 1 + RB, :]
            out = c0 * mid + c1 * pltpu.roll(mid, SIDE - 1, 1) + c2 * pltpu.roll(mid, 1, 1)
            out = out + c3 * nxt + c4 * prv
            new = jnp.clip(mid - prof[k] * out, 0.0, 1.0)
            state_out[0, k, rs, :] = new.astype(BF16)
            return acc + new

        total[rs, :] = lax.fori_loop(0, LV, move, jnp.zeros((RB, SIDE), F32), unroll=4)

    column = total[...] * (1.0 / scale) + Z_BOTTOM
    high = lax.Precision.HIGHEST
    packed = jnp.dot(column, down_l[0], preferred_element_type=F32, precision=high)
    packed = 0.25 * jnp.dot(down_r[...], packed, preferred_element_type=F32, precision=high)

    @pl.when(s == 0)
    def _():
        gathered[...] = packed

    @pl.when(s == 1)
    def _():
        coarse[...] = (gathered[...] + packed).astype(BF16).reshape(4, R, L)


def patches(foot, fraction):
    prof, weight, pick, rows, halves, down_l, down_r = patch_tables()
    full = lambda shape: pl.BlockSpec(shape, lambda s: (0,) * len(shape))
    return pl.pallas_call(
        patch_kernel,
        grid=(2,),
        out_shape=(
            jax.ShapeDtypeStruct((2, LV, SIDE, SIDE), BF16),
            jax.ShapeDtypeStruct((4, R, L), BF16),
        ),
        in_specs=[
            pl.BlockSpec(memory_space=pltpu.SMEM),
            pl.BlockSpec((1, 6, R, L), lambda s: (s, 0, 0, 0)),
            pl.BlockSpec((1, LV, SIDE, SIDE), lambda s: (s, 0, 0, 0)),
            full((SIDE, SIDE)),
            full((2, L, SIDE)),
            full((SIDE, TS)),
            full((2, SIDE, 32)),
            pl.BlockSpec((1, SIDE, L), lambda s: (s, 0, 0)),
            full((TS, SIDE)),
        ],
        out_specs=(
            pl.BlockSpec((1, LV, SIDE, SIDE), lambda s: (s, 0, 0, 0)),
            full((4, R, L)),
        ),
        scratch_shapes=[
            pltpu.VMEM((SIDE, SIDE), F32),
            pltpu.VMEM((5, SIDE, SIDE), F32),
            pltpu.VMEM((LV, SIDE + 2 * PAD, SIDE), F32),
            pltpu.VMEM((SIDE, SIDE), F32),
            pltpu.VMEM((TS, L), F32),
        ],
        compiler_params=pltpu.CompilerParams(
            dimension_semantics=("arbitrary",), vmem_limit_bytes=VMEM_LIMIT
        ),
        name="patches",
    )(prof, foot, fraction, weight, pick, rows, halves, down_l, down_r)


def fall_kernel(
    tiles, phys, coarse, tw_c, tw_s, spread, gather, bt_c, bt_s, finish,
    surface, tendency,
    source, tb, got, send, recv, out32,
    ssem, rsem, ssem2, rsem2,
):
    w = lax.axis_index("wide")
    g = lax.axis_index("grp")
    me = w * NG + g
    barrier = greet_all(me)

    row_of = 2 * w + g // 4
    for q in range(NG):
        want = row_of * 32 + 4 * q
        at = jnp.int32(0)
        for step in (16, 8, 4, 2, 1):
            at = at + jnp.where(tiles[q * 32 + at + step - 1] < want, step, 0)
        for c in range(4):
            found = tiles[q * 32 + at]
            cc = 4 * q + c
            source[0, cc] = jnp.bitwise_and(at, NW - 1) * NG + q
            source[1, cc] = lax.shift_right_logical(at, 4)
            source[2, cc] = jnp.where(found == want + c, 1, 0)
            at = jnp.minimum(at + jnp.where(found <= want + c, 1, 0), 31)

    pl.semaphore_wait(barrier, D - 1)
    pltpu.make_async_copy(coarse.at[g % 4], got.at[me], rsem).start()

    def post(k, carry):
        d = lax.rem(me + k, D)
        pltpu.make_async_remote_copy(
            coarse.at[d % 4], got.at[me], ssem, rsem, device_id=coords(d), device_id_type=MESH
        ).start()
        return carry

    lax.fori_loop(1, D, post, 0)
    pltpu.make_async_copy(got, got, rsem).wait()

    lane = lane_iota(R)
    low = lane < 64
    x = []
    for k2 in range(16):
        halves = []
        for h in range(2):
            cc = 2 * k2 + h
            tile = got[source[0, cc]].astype(F32)
            same = (lane * 0 + source[1, cc]) == h
            halves.append(jnp.where(same, tile, pltpu.roll(tile, 64, 1)))
        there = jnp.where(low, source[2, 2 * k2], source[2, 2 * k2 + 1]) == 1
        ht = phys[k2 * R:(k2 + 1) * R, :]
        vx = phys[256 + k2 * R:256 + (k2 + 1) * R, :]
        vy = phys[512 + k2 * R:512 + (k2 + 1) * R, :]
        sea = jnp.where(there, jnp.where(low, halves[0], halves[1]), ht)
        surface[:, k2 * L:(k2 + 1) * L] = sea
        x.append((-(sea + 0.5 * (vx * vx + vy * vy)), jnp.zeros((R, L), F32)))
    y = sixteenth(x, -1)
    for k1 in range(16):
        c, s = tw_c[k1:k1 + 1, :], tw_s[k1:k1 + 1, :]
        a, b = y[k1]
        re = (a * c - b * s).astype(BF16)
        im = (a * s + b * c).astype(BF16)
        q, e = k1 // 4, k1 % 4
        up = slice(e * R, (e + 1) * R)
        dn = slice(64 + e * R, 64 + (e + 1) * R)
        tb[q, up, 0:L] = re
        tb[q, up, L:2 * L] = -im
        tb[q, dn, 0:L] = im
        tb[q, dn, L:2 * L] = re

    for q in range(2):
        rhs = tb[2 * q:2 * q + 2].reshape(2 * L, 2 * L)
        z = nt_dot(spread[...], rhs)
        send[:, 2 * q, :] = z[:, :L]
        send[:, 2 * q + 1, :] = z[:, L:]

    pltpu.make_async_copy(send.at[me], recv.at[me], rsem2).start()

    def post2(k, carry):
        d = lax.rem(me + k, D)
        pltpu.make_async_remote_copy(
            send.at[d], recv.at[me], ssem2, rsem2, device_id=coords(d), device_id_type=MESH
        ).start()
        return carry

    lax.fori_loop(1, D, post2, 0)
    pltpu.make_async_copy(recv, recv, rsem2).wait()

    flip = jnp.where(lane_iota(D) < 64, -1.0, 1.0).astype(F32)
    for q in range(2):
        xx = jnp.concatenate(
            [recv[:, 2 * q, :].astype(BF16), recv[:, 2 * q + 1, :].astype(BF16)], axis=1
        )
        t = blocks_in(xx, gather[...], bt_c[...], bt_s[...], flip)
        out = nt_dot(finish[...], t) * (1.0 / N)
        for h in range(2):
            for c in range(2):
                for e in range(4):
                    r0 = (c * 4 + e) * R
                    out32[pl.ds(c * 256 + 8 * q + 4 * h + e, R, stride=R), :] = out[
                        r0:r0 + R, h * L:(h + 1) * L
                    ]
    for c in range(2):
        for k2 in range(16):
            at = c * 256 + k2 * R
            tendency[c, :, k2 * L:(k2 + 1) * L] = out32[at:at + R, :]

    pltpu.make_async_copy(got.at[pl.ds(0, D - 1)], got.at[pl.ds(0, D - 1)], ssem).wait()
    pltpu.make_async_copy(send.at[pl.ds(0, D - 1)], send.at[pl.ds(0, D - 1)], ssem2).wait()


def vmem(n):
    return [pl.BlockSpec(memory_space=pltpu.VMEM)] * n


def shards(eta_hat, phi_hat, patch_tiles, fraction):
    smem = pl.BlockSpec(memory_space=pltpu.SMEM)
    dma = pltpu.SemaphoreType.DMA
    phys, foot = pl.pallas_call(
        rise_kernel,
        out_shape=(
            jax.ShapeDtypeStruct((48 * R, L), F32),
            jax.ShapeDtypeStruct((2, 6, R, L), BF16),
        ),
        in_specs=[smem] + vmem(9),
        out_specs=tuple(vmem(2)),
        scratch_shapes=[
            pltpu.VMEM((16, L, 2 * L), BF16),
            pltpu.VMEM((D * R, L), F32),
            pltpu.VMEM((D, R, L), BF16),
            pltpu.VMEM((D, R, L), BF16),
            pltpu.VMEM((NG, 6, R, L), BF16),
            pltpu.VMEM((NG, 6, R, L), BF16),
            pltpu.VMEM((NW, 6, R, L), BF16),
            pltpu.VMEM((NW, 6, R, L), BF16),
        ] + [dma] * 6,
        compiler_params=pltpu.CompilerParams(
            collective_id=1, has_side_effects=True, vmem_limit_bytes=VMEM_LIMIT
        ),
        name="rise",
    )(patch_tiles, eta_hat, phi_hat, *lane_tables(1), *block_tables(1, 3, False))

    new_state, coarse = patches(foot, fraction[:, 0])

    surface, tendency = pl.pallas_call(
        fall_kernel,
        out_shape=(
            jax.ShapeDtypeStruct((R, N), F32),
            jax.ShapeDtypeStruct((2, R, N), F32),
        ),
        in_specs=[smem] + vmem(9),
        out_specs=tuple(vmem(2)),
        scratch_shapes=[
            pltpu.SMEM((3, 32), jnp.int32),
            pltpu.VMEM((4, L, 2 * L), BF16),
            pltpu.VMEM((D, R, L), BF16),
            pltpu.VMEM((D, 4, L), F32),
            pltpu.VMEM((D, 4, L), F32),
            pltpu.VMEM((512, L), F32),
        ] + [dma] * 4,
        compiler_params=pltpu.CompilerParams(
            collective_id=2, has_side_effects=True, vmem_limit_bytes=VMEM_LIMIT
        ),
        name="fall",
    )(patch_tiles, phys, coarse, *lane_tables(-1), *block_tables(-1, 4, True))
    return (surface, new_state[:, None], tendency)


def solution(mesh):
    placed = (
        P(None, ("wide", "grp"), None),
        P(None, ("wide", "grp"), None),
        P(),
        P(None, ("wide", "grp"), None, None, None),
    )
    return jax.shard_map(
        shards,
        mesh=mesh,
        in_specs=placed,
        out_specs=(
            P(("wide", "grp"), None),
            P(None, ("wide", "grp"), None, None, None),
            P(None, ("wide", "grp"), None),
        ),
        check_vma=False,
    )
```

time: 346 us -> 103 us (0.30); the launches traced: 339 us -> 103 us
  local copies, waits for them, and re-layouts: 104 us -> 3.24 us
  Pallas kernels: 0 us -> 99.3 us
  other arithmetic: 86.5 us -> 0 us
  waiting for transfers between devices: 53.3 us -> 0 us
  blocking collectives: 50.5 us -> 0 us
  starting transfers between devices: 16 us -> 0 us
  between operations: 15.4 us -> 0.65 us
  matrix products: 13 us -> 0 us
    pallas_call x0 -> x3, Pallas kernels: none -> 99.3 us  [the longest x1 39.7 us: shards(): pl.pallas_call(rise_kernel, out_shape=(jax.ShapeDtypeStruct((48 * R, L),...]
    add x7 -> x0, other arithmetic: 42.3 us -> none  [the longest x2 38.3 us: upwind_flux(): jnp.maximum(face_speed, 0.0) * left_vals]
    all_gather x1 -> x0, waiting for transfers between devices: 39.6 us -> none  [shards(): lax.all_gather(band_fields.astype(jnp.bfloat16), 'wide', axis=1, tiled=True)]
    slice x12 -> x0, local copies, waits for them, and re-layouts: 33.7 us -> none  [the longest x2 13.4 us: upwind_flux(): speed_pad = jnp.pad(speeds, widths, mode='edge')]
    all_to_all x2 -> x0, blocking collectives: 33.4 us -> none  [the longest x1 24.1 us: shards(): lax.all_to_all(inverse_rows, ('wide', 'grp'), split_axis=1, concat_axis=2...]
    broadcast_in_dim x1 -> x0, other arithmetic: 22 us -> none  [shards(): return (surface, new_states[:, None], tendency)]
    unnamed x33 -> x2, local copies, waits for them, and re-layouts: 21.2 us -> 3.24 us
    all_gather x1 -> x0, blocking collectives: 17.1 us -> none  [shards(): lax.all_gather(coarse_flat.reshape(2, 1, TS * TS).astype(jnp.bfloat16), '...]
  transfers between devices with their start and end apart: 3 -> 0, of which waited for: 3 -> 0; matrix products, arithmetic and copies ran while one was open for 2% -> 0% of each run, Pallas kernels for 0% -> 0%
where the time goes in v1:
time: 103 us
  Pallas kernels  99.3 us (96%)
  local copies, waits for them, and re-layouts  3.24 us (3%)
    pallas_call x1, Pallas kernels, shards(): pl.pallas_call(rise_kernel, out_shape=(jax.ShapeDtypeStruct((48 * R, L),...  39.7 us
    pallas_call x1, Pallas kernels, patches(): pl.pallas_call(patch_kernel, grid=(2,), out_shape=(jax.ShapeDtypeStruct((...  31.8 us
    pallas_call x1, Pallas kernels, shards(): pl.pallas_call(fall_kernel, out_shape=(jax.ShapeDtypeStruct((R, N), F32),...  27.8 us
    unnamed x2, local copies, waits for them, and re-layouts  3.24 us

profile of v1, /device:TPU:1, one launch (start us, length us, event | category | flops | bytes accessed | tf_op | source)
XLA Modules:
  0.0 103.2 jit_solution(16464208324309550328)
XLA Ops:
  0.6 39.7 %rise.1 = (f32[768,128]{1,0:T(8,128)}, bf16[2,6,16,128]{3,2,1,0:T(8,128)(2,1)}) custom-call(s32[256]{0:T(256)} %tiles.3, bf16[2,16,2048]{2,1,0:T(8,128)(2,1)} %eta.1, bf16[2,16,2048]{2,1,0:T(8,128)(2,1)} %phi.1, f32[16,128]{1,0:T(8,128)} %constant.38.clone.tw_c, f32[16,128]{1,0:T(8,128)} %constant.39.clone.tw_s, bf16[128,256]{1,0:T(8,128)(2,1)} %constant.60.spread, ...), custom_call_target="tpu_custom_call" | custom-call | tf_op jit(solution)/shard_map/rise/pallas_call | solution.py:597
  40.4 31.8 %patches.1 = (bf16[2,64,128,128]{3,2,1,0:T(8,128)(2,1)}, bf16[4,16,128]{2,1,0:T(8,128)(2,1)}) custom-call(f32[64]{0:T(128)} %constant.45.clone.prof, bf16[2,6,16,128]{3,2,1,0:T(8,128)(2,1)} %get-tuple-element.10.foot, bf16[2,64,128,128]{3,2,1,0:T(8,128)(2,1)} %bitcast.4, f32[128,128]{1,0:T(8,128)} %constant.46.clone.weight, ...), custom_call_target="tpu_custom_call" | custom-call | tf_op jit(solution)/shard_map/patches/pallas_call | solution.py:444
  72.2 27.8 %fall.1 = (f32[16,2048]{1,0:T(8,128)}, f32[2,16,2048]{2,1,0:T(8,128)}) custom-call(s32[256]{0:T(256)} %tiles.3, f32[768,128]{1,0:T(8,128)} %get-tuple-element.9.phys, bf16[4,16,128]{2,1,0:T(8,128)(2,1)} %get-tuple-element.11.coarse, f32[16,128]{1,0:T(8,128)} %constant.38.clone.tw_c, f32[16,128]{1,0:T(8,128)} %constant.52.clone.tw_s, ...), custom_call_target="tpu_custom_call" | custom-call | tf_op jit(solution)/shard_map/fall/pallas_call | solution.py:623
  99.9 1.6 %copy.31 = f32[16,2048]{1,0:T(8,128)} copy(f32[16,2048]{1,0:T(8,128)} %get-tuple-element.21) | data formatting | bytes 262144
  101.5 1.7 %copy.32 = f32[2,16,2048]{2,1,0:T(8,128)} copy(f32[2,16,2048]{2,1,0:T(8,128)} %get-tuple-element.23) | data formatting | bytes 524288

commit v2 on v1

--- a/solution.py
+++ b/solution.py
@@ -34,12 +34,14 @@
     return np.cos(angle), np.sin(angle)
 
 
-def lane_tables(sign):
+def lane_tables(sign, by_group):
     k1 = np.arange(R)[:, None]
     n2 = np.arange(L)[None, :]
     tc, ts = unit(k1 * n2, N)
-    k2 = np.arange(D)[:, None]
-    c, s = unit(k2 * n2, D)
+    k2 = np.arange(D)
+    if by_group:
+        k2 = k2.reshape(NW, NG).T.reshape(-1)
+    c, s = unit(k2[:, None] * n2, D)
     spread = np.concatenate([c, sign * s], axis=1)
     return (
         jnp.asarray(tc, F32),
@@ -204,7 +206,7 @@
         wide32[pl.ds(2 * kk + 1, D, stride=R), :] = z[:, L:]
         return carry
 
-    lax.fori_loop(0, 8, rows_out, 0)
+    lax.fori_loop(0, 8, rows_out, 0, unroll=2)
 
     def narrow(i, carry):
         part = wide32[pl.ds(pl.multiple_of(i * 128, 128), 128), :]
@@ -249,7 +251,7 @@
         phys[pl.ds(2 * yy + 1, 48, stride=R), :] = out[:, L:]
         return carry
 
-    lax.fori_loop(0, 8, columns, 0)
+    lax.fori_loop(0, 8, columns, 0, unroll=4)
 
     low = lane < 64
 
@@ -264,7 +266,7 @@
             send1[q, 3 + 2 * h] = jnp.where(low, pltpu.roll(vx, 64, 1), vy).astype(BF16)
         return carry
 
-    lax.fori_loop(0, NG, by_group, 0)
+    lax.fori_loop(0, NG, by_group, 0, unroll=2)
 
     pltpu.make_async_copy(send1.at[g], recv1.at[g], rsem1).start()
     for k in range(1, NG):
@@ -338,200 +340,226 @@
         jnp.asarray(pick, F32).astype(BF16),
         jnp.asarray(rows, F32).astype(BF16),
         jnp.asarray(halves, F32).astype(BF16),
-        jnp.asarray(np.swapaxes(pick, 1, 2), F32),
-        jnp.asarray(rows.T, F32),
     )
 
 
 RB = 16
 PAD = 8
+STEP = 16
+TOGETHER = 8
 
 
 def patch_kernel(
-    prof, foot, state, weight, pick, rows, halves, down_l, down_r,
+    prof, foot, state, weight, pick, rows, halves, down_rows, down_cols,
     state_out, coarse,
-    hh, cf, bl, total, gathered,
+    hh, cf, bl, total,
 ):
-    s = pl.program_id(0)
-
-    vel = foot[0, 0:4].reshape(64, L)
-    hgt = foot[0, 4:6].reshape(32, L)
-
-    def up(m, sel, spread_rows):
-        wide = jnp.dot(m, sel, preferred_element_type=F32).astype(BF16)
-        return jnp.dot(spread_rows, wide, preferred_element_type=F32)
-
-    height = up(hgt, pick[0], halves[0]) + up(hgt, pick[1], halves[1])
-    ax = up(vel, pick[0], rows[...])
-    ay = up(vel, pick[1], rows[...])
+    j = pl.program_id(1)
     scale = LV / (Z_TOP - Z_BOTTOM)
-    hh[...] = height * scale - Z_BOTTOM * scale
-
-    lane = lax.broadcasted_iota(jnp.int32, (SIDE, SIDE), 1)
-    sub = lax.broadcasted_iota(jnp.int32, (SIDE, SIDE), 0)
-
-    def faces(a, axis, index):
-        after = jnp.where(index == SIDE - 1, a, pltpu.roll(a, SIDE - 1, axis))
-        before = jnp.where(index == 0, a, pltpu.roll(a, 1, axis))
-        return (0.5 * COURANT) * (a + after), (0.5 * COURANT) * (before + a)
-
-    center = jnp.zeros((SIDE, SIDE), F32)
-    for n, (a, axis, index) in enumerate(((ax, 1, lane), (ay, 0, sub))):
-        upper, lower = faces(a, axis, index)
-        center += jnp.maximum(upper, 0.0) - jnp.minimum(lower, 0.0)
-        from_up = jnp.minimum(upper, 0.0)
-        from_low = -jnp.maximum(lower, 0.0)
-        last, first = index == SIDE - 1, index == 0
-        center += jnp.where(last, from_up, 0.0) + jnp.where(first, from_low, 0.0)
-        cf[1 + 2 * n] = jnp.where(last, 0.0, from_up)
-        cf[2 + 2 * n] = jnp.where(first, 0.0, from_low)
-    cf[0] = center
-
-    edge = jnp.zeros((PAD, SIDE), F32)
-    for b in range(SIDE // RB):
-        rs = slice(b * RB, (b + 1) * RB)
-        h = hh[rs, :]
-        wt = weight[rs, :]
-        keep = 1.0 - wt
-
-        def blend(k, carry, b=b, rs=rs, h=h, wt=wt, keep=keep):
-            sea = jnp.clip(h - k.astype(F32), 0.0, 1.0)
-            bl[k, PAD + b * RB:PAD + (b + 1) * RB, :] = (
-                wt * sea + keep * state[0, k, rs, :].astype(F32)
-            )
-            if b == 0:
-                bl[k, 0:PAD, :] = edge
-            if b == SIDE // RB - 1:
-                bl[k, PAD + SIDE:, :] = edge
-            return carry
-
-        lax.fori_loop(0, LV, blend, 0, unroll=4)
-
-    for b in range(SIDE // RB):
-        rs = slice(b * RB, (b + 1) * RB)
-        at = PAD + b * RB
-        c0, c1, c2, c3, c4 = (cf[n, rs, :] for n in range(5))
-
-        def move(k, acc, at=at, rs=rs, c0=c0, c1=c1, c2=c2, c3=c3, c4=c4):
-            mid = bl[k, at:at + RB, :]
-            nxt = bl[k, at + 1:at + 1 + RB, :]
-            prv = bl[k, at - 1:at - 1 + RB, :]
-            out = c0 * mid + c1 * pltpu.roll(mid, SIDE - 1, 1) + c2 * pltpu.roll(mid, 1, 1)
-            out = out + c3 * nxt + c4 * prv
-            new = jnp.clip(mid - prof[k] * out, 0.0, 1.0)
-            state_out[0, k, rs, :] = new.astype(BF16)
-            return acc + new
-
-        total[rs, :] = lax.fori_loop(0, LV, move, jnp.zeros((RB, SIDE), F32), unroll=4)
-
-    column = total[...] * (1.0 / scale) + Z_BOTTOM
-    high = lax.Precision.HIGHEST
-    packed = jnp.dot(column, down_l[0], preferred_element_type=F32, precision=high)
-    packed = 0.25 * jnp.dot(down_r[...], packed, preferred_element_type=F32, precision=high)
-
-    @pl.when(s == 0)
+
+    @pl.when(j == 0)
     def _():
-        gathered[...] = packed
-
-    @pl.when(s == 1)
+        vel = foot[0, 0:4].reshape(64, L)
+        hgt = foot[0, 4:6].reshape(32, L)
+
+        def up(m, sel, spread_rows):
+            wide = jnp.dot(m, sel, preferred_element_type=F32).astype(BF16)
+            return jnp.dot(spread_rows, wide, preferred_element_type=F32)
+
+        height = up(hgt, pick[0], halves[0]) + up(hgt, pick[1], halves[1])
+        ax = up(vel, pick[0], rows[...])
+        ay = up(vel, pick[1], rows[...])
+        hh[...] = height * scale - Z_BOTTOM * scale
+
+        lane = lax.broadcasted_iota(jnp.int32, (SIDE, SIDE), 1)
+        sub = lax.broadcasted_iota(jnp.int32, (SIDE, SIDE), 0)
+
+        def faces(a, axis, index):
+            after = jnp.where(index == SIDE - 1, a, pltpu.roll(a, SIDE - 1, axis))
+            before = jnp.where(index == 0, a, pltpu.roll(a, 1, axis))
+            return (0.5 * COURANT) * (a + after), (0.5 * COURANT) * (before + a)
+
+        center = jnp.zeros((SIDE, SIDE), F32)
+        for n, (a, axis, index) in enumerate(((ax, 1, lane), (ay, 0, sub))):
+            upper, lower = faces(a, axis, index)
+            center += jnp.maximum(upper, 0.0) - jnp.minimum(lower, 0.0)
+            from_up = jnp.minimum(upper, 0.0)
+            from_low = -jnp.maximum(lower, 0.0)
+            last, first = index == SIDE - 1, index == 0
+            center += jnp.where(last, from_up, 0.0) + jnp.where(first, from_low, 0.0)
+            cf[1 + 2 * n] = jnp.where(last, 0.0, from_up)
+            cf[2 + 2 * n] = jnp.where(first, 0.0, from_low)
+        cf[0] = center
+        total[...] = jnp.zeros((SIDE, SIDE), F32)
+        edge = jnp.zeros((TOGETHER, PAD, SIDE), F32)
+        bl[:, 0:PAD, :] = edge
+        bl[:, PAD + SIDE:, :] = edge
+
+    def group(i, carry):
+        for b in range(SIDE // RB):
+            rs = slice(b * RB, (b + 1) * RB)
+            h, wt = hh[rs, :], weight[rs, :]
+            keep = 1.0 - wt
+            for l in range(TOGETHER):
+                here = i * TOGETHER + l
+                sea = jnp.clip(h - (j * STEP + here).astype(F32), 0.0, 1.0)
+                bl[l, PAD + b * RB:PAD + (b + 1) * RB, :] = (
+                    wt * sea + keep * state[0, here, rs, :].astype(F32)
+                )
+        for b in range(SIDE // RB):
+            rs = slice(b * RB, (b + 1) * RB)
+            at = PAD + b * RB
+            c0, c1, c2, c3, c4 = (cf[n, rs, :] for n in range(5))
+            acc = total[rs, :]
+            for l in range(TOGETHER):
+                here = i * TOGETHER + l
+                mid = bl[l, at:at + RB, :]
+                nxt = bl[l, at + 1:at + 1 + RB, :]
+                prv = bl[l, at - 1:at - 1 + RB, :]
+                out = c0 * mid + c1 * pltpu.roll(mid, SIDE - 1, 1) + c2 * pltpu.roll(mid, 1, 1)
+                out = out + c3 * nxt + c4 * prv
+                new = jnp.clip(mid - prof[j * STEP + here] * out, 0.0, 1.0)
+                state_out[0, here, rs, :] = new.astype(BF16)
+                acc = acc + new
+            total[rs, :] = acc
+        return carry
+
+    lax.fori_loop(0, STEP // TOGETHER, group, 0)
+
+    @pl.when(j == LV // STEP - 1)
     def _():
-        coarse[...] = (gathered[...] + packed).astype(BF16).reshape(4, R, L)
+        column = total[...] * (1.0 / scale) + Z_BOTTOM
+        high = lax.Precision.HIGHEST
+
+        def down(h):
+            part = jnp.dot(down_rows[h], column, preferred_element_type=F32, precision=high)
+            return jnp.dot(part, down_cols[h], preferred_element_type=F32, precision=high)
+
+        coarse[0] = (0.25 * (down(0) + down(1))).astype(BF16).reshape(2, R, L)
 
 
 def patches(foot, fraction):
-    prof, weight, pick, rows, halves, down_l, down_r = patch_tables()
-    full = lambda shape: pl.BlockSpec(shape, lambda s: (0,) * len(shape))
+    prof, weight, pick, rows, halves = patch_tables()
+    down_rows = jnp.swapaxes(halves, 1, 2).astype(F32)
+    down_cols = jnp.swapaxes(pick, 1, 2).astype(F32)
+    full = lambda shape: pl.BlockSpec(shape, lambda s, j: (0,) * len(shape))
+    levels = pl.BlockSpec((1, STEP, SIDE, SIDE), lambda s, j: (s, j, 0, 0))
     return pl.pallas_call(
         patch_kernel,
-        grid=(2,),
+        grid=(2, LV // STEP),
         out_shape=(
             jax.ShapeDtypeStruct((2, LV, SIDE, SIDE), BF16),
-            jax.ShapeDtypeStruct((4, R, L), BF16),
+            jax.ShapeDtypeStruct((2, 2, R, L), BF16),
         ),
         in_specs=[
             pl.BlockSpec(memory_space=pltpu.SMEM),
-            pl.BlockSpec((1, 6, R, L), lambda s: (s, 0, 0, 0)),
-            pl.BlockSpec((1, LV, SIDE, SIDE), lambda s: (s, 0, 0, 0)),
+            pl.BlockSpec((1, 6, R, L), lambda s, j: (s, 0, 0, 0)),
+            levels,
             full((SIDE, SIDE)),
             full((2, L, SIDE)),
             full((SIDE, TS)),
             full((2, SIDE, 32)),
-            pl.BlockSpec((1, SIDE, L), lambda s: (s, 0, 0)),
-            full((TS, SIDE)),
+            full((2, 32, SIDE)),
+            full((2, SIDE, L)),
         ],
-        out_specs=(
-            pl.BlockSpec((1, LV, SIDE, SIDE), lambda s: (s, 0, 0, 0)),
-            full((4, R, L)),
-        ),
+        out_specs=(levels, pl.BlockSpec((1, 2, R, L), lambda s, j: (s, 0, 0, 0))),
         scratch_shapes=[
             pltpu.VMEM((SIDE, SIDE), F32),
             pltpu.VMEM((5, SIDE, SIDE), F32),
-            pltpu.VMEM((LV, SIDE + 2 * PAD, SIDE), F32),
+            pltpu.VMEM((TOGETHER, SIDE + 2 * PAD, SIDE), F32),
             pltpu.VMEM((SIDE, SIDE), F32),
-            pltpu.VMEM((TS, L), F32),
         ],
         compiler_params=pltpu.CompilerParams(
-            dimension_semantics=("arbitrary",), vmem_limit_bytes=VMEM_LIMIT
+            dimension_semantics=("arbitrary", "arbitrary"), vmem_limit_bytes=VMEM_LIMIT
         ),
         name="patches",
-    )(prof, foot, fraction, weight, pick, rows, halves, down_l, down_r)
+    )(prof, foot, fraction, weight, pick, rows, halves, down_rows, down_cols)
+
+
+def rank_of(tiles, q, want):
+    at = jnp.int32(0)
+    for step in (16, 8, 4, 2, 1):
+        at = at + jnp.where(tiles[q * 32 + at + step - 1] < want, step, 0)
+    return at
 
 
 def fall_kernel(
     tiles, phys, coarse, tw_c, tw_s, spread, gather, bt_c, bt_s, finish,
-    surface, tendency,
-    source, tb, got, send, recv, out32,
-    ssem, rsem, ssem2, rsem2,
+    out,
+    source, tb, block, got1, strip, got2, send1, recv1, rows32, send2, recv2, cols32, out32,
+    bsem, bsem2, csem1, dsem1, csem2, dsem2, csem3, dsem3,
 ):
     w = lax.axis_index("wide")
     g = lax.axis_index("grp")
-    me = w * NG + g
-    barrier = greet_all(me)
-
-    row_of = 2 * w + g // 4
+    barrier = pltpu.get_barrier_semaphore()
+    for k in range(1, NG):
+        pl.semaphore_signal(
+            barrier, inc=1, device_id=(w, lax.rem(g + k, NG)), device_id_type=MESH
+        )
+    for k in range(1, NW):
+        pl.semaphore_signal(
+            barrier, inc=1, device_id=(lax.rem(w + k, NW), g), device_id_type=MESH
+        )
+
+    first = lax.shift_right_logical(tiles[g * 32 + w], 6)
+    for d in range(NW):
+        slot = jnp.where(first == d, 0, 1)
+        for p in range(2):
+            block[d, p] = coarse[slot, p]
+
+    pl.semaphore_wait(barrier, NG + NW - 2)
+
+    pltpu.make_async_copy(block.at[w], got1.at[w], csem1).start()
+    for k in range(1, NW):
+        d = lax.rem(w + k, NW)
+        pltpu.make_async_remote_copy(
+            block.at[d], got1.at[w], bsem, csem1, device_id=(d, g), device_id_type=MESH
+        ).start()
+
+    for upper in range(2):
+        want = (2 * w + upper) * 32 + 4 * g
+        at = rank_of(tiles, g, want)
+        for c in range(4):
+            source[0, 4 * upper + c] = jnp.bitwise_and(at, NW - 1)
+            at = jnp.minimum(at + jnp.where(tiles[g * 32 + at] <= want + c, 1, 0), 31)
     for q in range(NG):
-        want = row_of * 32 + 4 * q
-        at = jnp.int32(0)
-        for step in (16, 8, 4, 2, 1):
-            at = at + jnp.where(tiles[q * 32 + at + step - 1] < want, step, 0)
+        want = (2 * w + g // 4) * 32 + 4 * q
+        at = rank_of(tiles, q, want)
         for c in range(4):
             found = tiles[q * 32 + at]
-            cc = 4 * q + c
-            source[0, cc] = jnp.bitwise_and(at, NW - 1) * NG + q
-            source[1, cc] = lax.shift_right_logical(at, 4)
-            source[2, cc] = jnp.where(found == want + c, 1, 0)
+            source[1, 4 * q + c] = jnp.where(found == want + c, 1, 0)
             at = jnp.minimum(at + jnp.where(found <= want + c, 1, 0), 31)
-
-    pl.semaphore_wait(barrier, D - 1)
-    pltpu.make_async_copy(coarse.at[g % 4], got.at[me], rsem).start()
-
-    def post(k, carry):
-        d = lax.rem(me + k, D)
-        pltpu.make_async_remote_copy(
-            coarse.at[d % 4], got.at[me], ssem, rsem, device_id=coords(d), device_id_type=MESH
-        ).start()
-        return carry
-
-    lax.fori_loop(1, D, post, 0)
-    pltpu.make_async_copy(got, got, rsem).wait()
 
     lane = lane_iota(R)
     low = lane < 64
+    pltpu.make_async_copy(got1, got1, csem1).wait()
+
+    for q in range(NG):
+        upper, rb = q // 4, q % 4
+        for p in range(2):
+            sides = []
+            for h in range(2):
+                tile = got1[source[0, 4 * upper + 2 * p + h], rb // 2].astype(F32)
+                sides.append(tile if rb % 2 == h else pltpu.roll(tile, 64, 1))
+            strip[q, p] = jnp.where(low, sides[0], sides[1]).astype(BF16)
+
+    pltpu.make_async_copy(strip.at[g], got2.at[g], csem2).start()
+    for k in range(1, NG):
+        d = lax.rem(g + k, NG)
+        pltpu.make_async_remote_copy(
+            strip.at[d], got2.at[g], dsem1, csem2, device_id=(w, d), device_id_type=MESH
+        ).start()
+    pltpu.make_async_copy(got2, got2, csem2).wait()
+
     x = []
     for k2 in range(16):
-        halves = []
-        for h in range(2):
-            cc = 2 * k2 + h
-            tile = got[source[0, cc]].astype(F32)
-            same = (lane * 0 + source[1, cc]) == h
-            halves.append(jnp.where(same, tile, pltpu.roll(tile, 64, 1)))
-        there = jnp.where(low, source[2, 2 * k2], source[2, 2 * k2 + 1]) == 1
+        there = jnp.where(low, source[1, 2 * k2], source[1, 2 * k2 + 1]) == 1
         ht = phys[k2 * R:(k2 + 1) * R, :]
         vx = phys[256 + k2 * R:256 + (k2 + 1) * R, :]
         vy = phys[512 + k2 * R:512 + (k2 + 1) * R, :]
-        sea = jnp.where(there, jnp.where(low, halves[0], halves[1]), ht)
-        surface[:, k2 * L:(k2 + 1) * L] = sea
-        x.append((-(sea + 0.5 * (vx * vx + vy * vy)), jnp.zeros((R, L), F32)))
+        sea = -jnp.where(there, got2[k2 // 2, k2 % 2].astype(F32), ht)
+        out[0, :, k2 * L:(k2 + 1) * L] = sea
+        x.append((sea - 0.5 * (vx * vx + vy * vy), jnp.zeros((R, L), F32)))
     y = sixteenth(x, -1)
     for k1 in range(16):
         c, s = tw_c[k1:k1 + 1, :], tw_s[k1:k1 + 1, :]
@@ -548,43 +576,62 @@
 
     for q in range(2):
         rhs = tb[2 * q:2 * q + 2].reshape(2 * L, 2 * L)
-        z = nt_dot(spread[...], rhs)
-        send[:, 2 * q, :] = z[:, :L]
-        send[:, 2 * q + 1, :] = z[:, L:]
-
-    pltpu.make_async_copy(send.at[me], recv.at[me], rsem2).start()
-
-    def post2(k, carry):
-        d = lax.rem(me + k, D)
+        z = nt_dot(spread[...], rhs).astype(BF16)
+        for h in range(2):
+            for d in range(NG):
+                send1[d, 2 * q + h] = z[d * NW:(d + 1) * NW, h * L:(h + 1) * L]
+
+    pltpu.make_async_copy(send1.at[g], recv1.at[g], csem3).start()
+    for k in range(1, NG):
+        d = lax.rem(g + k, NG)
         pltpu.make_async_remote_copy(
-            send.at[d], recv.at[me], ssem2, rsem2, device_id=coords(d), device_id_type=MESH
+            send1.at[d], recv1.at[g], dsem2, csem3, device_id=(w, d), device_id_type=MESH
         ).start()
-        return carry
-
-    lax.fori_loop(1, D, post2, 0)
-    pltpu.make_async_copy(recv, recv, rsem2).wait()
-
+    pltpu.make_async_copy(recv1, recv1, csem3).wait()
+
+    rows32[...] = recv1[...].astype(F32).reshape(4 * NG * NW, L)
+    for d in range(NW):
+        send2[d] = rows32[pl.ds(d, 4 * NG, stride=NW), :].astype(BF16).reshape(2, R, L)
+
+    pltpu.make_async_copy(send2.at[w], recv2.at[w], dsem3).start()
+    for k in range(1, NW):
+        d = lax.rem(w + k, NW)
+        pltpu.make_async_remote_copy(
+            send2.at[d], recv2.at[w], bsem2, dsem3, device_id=(d, g), device_id_type=MESH
+        ).start()
+    pltpu.make_async_copy(recv2, recv2, dsem3).wait()
+
+    cols32[...] = recv2[...].astype(F32).reshape(4 * D, L)
     flip = jnp.where(lane_iota(D) < 64, -1.0, 1.0).astype(F32)
     for q in range(2):
         xx = jnp.concatenate(
-            [recv[:, 2 * q, :].astype(BF16), recv[:, 2 * q + 1, :].astype(BF16)], axis=1
+            [
+                cols32[pl.ds(2 * q, D, stride=4), :].astype(BF16),
+                cols32[pl.ds(2 * q + 1, D, stride=4), :].astype(BF16),
+            ],
+            axis=1,
         )
         t = blocks_in(xx, gather[...], bt_c[...], bt_s[...], flip)
-        out = nt_dot(finish[...], t) * (1.0 / N)
+        done = nt_dot(finish[...], t)
         for h in range(2):
             for c in range(2):
                 for e in range(4):
                     r0 = (c * 4 + e) * R
-                    out32[pl.ds(c * 256 + 8 * q + 4 * h + e, R, stride=R), :] = out[
+                    out32[pl.ds(c * 256 + 8 * q + 4 * h + e, R, stride=R), :] = done[
                         r0:r0 + R, h * L:(h + 1) * L
                     ]
     for c in range(2):
         for k2 in range(16):
             at = c * 256 + k2 * R
-            tendency[c, :, k2 * L:(k2 + 1) * L] = out32[at:at + R, :]
-
-    pltpu.make_async_copy(got.at[pl.ds(0, D - 1)], got.at[pl.ds(0, D - 1)], ssem).wait()
-    pltpu.make_async_copy(send.at[pl.ds(0, D - 1)], send.at[pl.ds(0, D - 1)], ssem2).wait()
+            out[1 + c, :, k2 * L:(k2 + 1) * L] = out32[at:at + R, :]
+
+    def sent(buf, n, sem):
+        pltpu.make_async_copy(buf.at[pl.ds(0, n)], buf.at[pl.ds(0, n)], sem).wait()
+
+    sent(block, NW - 1, bsem)
+    sent(send2, NW - 1, bsem2)
+    sent(strip, NG - 1, dsem1)
+    sent(send1, NG - 1, dsem2)
 
 
 def vmem(n):
@@ -616,32 +663,36 @@
             collective_id=1, has_side_effects=True, vmem_limit_bytes=VMEM_LIMIT
         ),
         name="rise",
-    )(patch_tiles, eta_hat, phi_hat, *lane_tables(1), *block_tables(1, 3, False))
+    )(patch_tiles, eta_hat, phi_hat, *lane_tables(1, False), *block_tables(1, 3, False))
 
     new_state, coarse = patches(foot, fraction[:, 0])
 
-    surface, tendency = pl.pallas_call(
+    fallen = pl.pallas_call(
         fall_kernel,
-        out_shape=(
-            jax.ShapeDtypeStruct((R, N), F32),
-            jax.ShapeDtypeStruct((2, R, N), F32),
-        ),
+        out_shape=jax.ShapeDtypeStruct((3, R, N), F32),
         in_specs=[smem] + vmem(9),
-        out_specs=tuple(vmem(2)),
+        out_specs=vmem(1)[0],
         scratch_shapes=[
-            pltpu.SMEM((3, 32), jnp.int32),
+            pltpu.SMEM((2, 32), jnp.int32),
             pltpu.VMEM((4, L, 2 * L), BF16),
-            pltpu.VMEM((D, R, L), BF16),
-            pltpu.VMEM((D, 4, L), F32),
-            pltpu.VMEM((D, 4, L), F32),
+            pltpu.VMEM((NW, 2, R, L), BF16),
+            pltpu.VMEM((NW, 2, R, L), BF16),
+            pltpu.VMEM((NG, 2, R, L), BF16),
+            pltpu.VMEM((NG, 2, R, L), BF16),
+            pltpu.VMEM((NG, 4, NW, L), BF16),
+            pltpu.VMEM((NG, 4, NW, L), BF16),
+            pltpu.VMEM((4 * NG * NW, L), F32),
+            pltpu.VMEM((NW, 2, R, L), BF16),
+            pltpu.VMEM((NW, 2, R, L), BF16),
+            pltpu.VMEM((4 * D, L), F32),
             pltpu.VMEM((512, L), F32),
-        ] + [dma] * 4,
+        ] + [dma] * 8,
         compiler_params=pltpu.CompilerParams(
             collective_id=2, has_side_effects=True, vmem_limit_bytes=VMEM_LIMIT
         ),
         name="fall",
-    )(patch_tiles, phys, coarse, *lane_tables(-1), *block_tables(-1, 4, True))
-    return (surface, new_state[:, None], tendency)
+    )(patch_tiles, phys, coarse, *lane_tables(-1, True), *block_tables(-1, 4, True))
+    return (-fallen[0], new_state[:, None], fallen[1:] * (1.0 / N))
 
 
 def solution(mesh):

time: 103 us -> 79.3 us (0.77)
  Pallas kernels: 99.3 us -> 75 us
  other arithmetic: 0 us -> 3.24 us
  local copies, waits for them, and re-layouts: 3.24 us -> 0 us
    pallas_call x2, Pallas kernels: 59.5 us -> 36.5 us  [the longest x1 24.8 us: shards(): pl.pallas_call(fall_kernel, out_shape=jax.ShapeDtypeStruct((3, R, N), F32...]
    unnamed x2 -> x0, local copies, waits for them, and re-layouts: 3.24 us -> none
    mul x0 -> x1, other arithmetic: none -> 1.67 us  [shards(): return (-fallen[0], new_state[:, None], fallen[1:] * (1.0 / N))]
    neg x0 -> x1, other arithmetic: none -> 1.57 us  [shards(): return (-fallen[0], new_state[:, None], fallen[1:] * (1.0 / N))]
    pallas_call x1, Pallas kernels: 39.7 us -> 38.6 us  [shards(): pl.pallas_call(rise_kernel, out_shape=(jax.ShapeDtypeStruct((48 * R, L),...]
where the time goes in v2:
time: 79.3 us; the launch traced here: 78.9 us
  Pallas kernels  75 us (95%)
  other arithmetic  3.24 us (4%)
    pallas_call x1, Pallas kernels, shards(): pl.pallas_call(rise_kernel, out_shape=(jax.ShapeDtypeStruct((48 * R, L),...  38.6 us
    pallas_call x1, Pallas kernels, shards(): pl.pallas_call(fall_kernel, out_shape=jax.ShapeDtypeStruct((3, R, N), F32...  24.8 us
    pallas_call x1, Pallas kernels, patches(): pl.pallas_call(patch_kernel, grid=(2, LV // STEP), out_shape=(jax.ShapeDt...  11.7 us
    mul x1, other arithmetic, shards(): return (-fallen[0], new_state[:, None], fallen[1:] * (1.0 / N))  1.67 us

profile of v2, /device:TPU:1, one launch (start us, length us, event | category | flops | bytes accessed | tf_op | source)
XLA Modules:
  0.0 78.9 jit_solution(3375290575409554130)
XLA Ops:
  0.6 38.6 %rise.1 = (f32[768,128]{1,0:T(8,128)}, bf16[2,6,16,128]{3,2,1,0:T(8,128)(2,1)}) custom-call(s32[256]{0:T(256)} %tiles.3, bf16[2,16,2048]{2,1,0:T(8,128)(2,1)} %eta.1, bf16[2,16,2048]{2,1,0:T(8,128)(2,1)} %phi.1, f32[16,128]{1,0:T(8,128)} %constant.36.clone.tw_c, f32[16,128]{1,0:T(8,128)} %constant.37.clone.tw_s, bf16[128,256]{1,0:T(8,128)(2,1)} %constant.56.spread, ...), custom_call_target="tpu_custom_call" | custom-call | tf_op jit(solution)/shard_map/rise/pallas_call | solution.py:644
  39.2 11.7 %patches.1 = (bf16[2,64,128,128]{3,2,1,0:T(8,128)(2,1)}, bf16[2,2,16,128]{3,2,1,0:T(8,128)(2,1)}) custom-call(f32[64]{0:T(128)} %constant.43.clone.prof, bf16[2,6,16,128]{3,2,1,0:T(8,128)(2,1)} %get-tuple-element.8.foot, bf16[2,64,128,128]{3,2,1,0:T(8,128)(2,1)} %bitcast.6, f32[128,128]{1,0:T(8,128)} %constant.44.clone.weight, ...), custom_call_target="tpu_custom_call" | custom-call | tf_op jit(solution)/shard_map/patches/pallas_call | solution.py:447
  50.9 24.8 %fall.1 = f32[3,16,2048]{2,1,0:T(8,128)} custom-call(s32[256]{0:T(256)} %tiles.3, f32[768,128]{1,0:T(8,128)} %get-tuple-element.7.phys, bf16[2,2,16,128]{3,2,1,0:T(8,128)(2,1)} %get-tuple-element.9.coarse, f32[16,128]{1,0:T(8,128)} %constant.36.clone.tw_c, f32[16,128]{1,0:T(8,128)} %constant.48.clone.tw_s, bf16[128,256]{1,0:T(8,128)(2,1)} %constant.66.spread, ...), custom_call_target="tpu_custom_call" | custom-call | tf_op jit(solution)/shard_map/fall/pallas_call | solution.py:670
  75.7 1.6 %negate_bitcast_fusion = f32[16,2048]{1,0:T(8,128)} fusion(f32[3,16,2048]{2,1,0:T(8,128)} %fall.1), kind=kLoop, calls=%fused_computation.1 | loop fusion | flops 32768 | bytes 262144 | tf_op jit(solution)/shard_map/neg | solution.py:695
  77.3 1.7 %slice_multiply_fusion = f32[2,16,2048]{2,1,0:T(8,128)} fusion(f32[3,16,2048]{2,1,0:T(8,128)} %fall.1), kind=kLoop, calls=%fused_computation | loop fusion | flops 65536 | bytes 524288 | tf_op jit(solution)/shard_map/mul | solution.py:695

commit v3 on v1

v3 whole, which is shorter than its diff:
```python
import functools
import math

import jax
import jax.numpy as jnp
import numpy as np
from jax import lax
from jax.experimental import pallas as pl
from jax.experimental.pallas import tpu as pltpu
from jax.sharding import PartitionSpec as P

F32 = jnp.float32
BF16 = jnp.bfloat16
MESH = pl.DeviceIdType.MESH

N = 2048
D = 128
NW = 16
NG = 8
L = 128
R = 16
LV = 64
SIDE = 128
TS = 64
Z_BOTTOM = -2.0
Z_TOP = 2.0
DECAY_RATE = 0.5
COURANT = 0.3
VMEM_LIMIT = 56 << 20


def unit(phase, length):
    angle = (phase % length) * (2.0 * math.pi / length)
    return np.cos(angle), np.sin(angle)


def lane_tables(sign):
    k1 = np.arange(R)[:, None]
    n2 = np.arange(L)[None, :]
    tc, ts = unit(k1 * n2, N)
    k2 = np.arange(D)[:, None]
    c, s = unit(k2 * n2, D)
    spread = np.concatenate([c, sign * s], axis=1)
    return (
        jnp.asarray(tc, F32),
        jnp.asarray(sign * ts, F32),
        jnp.asarray(spread, F32).astype(BF16),
    )


def block_tables(sign, blocks, full):
    k1 = np.arange(D)[:, None]
    src = np.arange(D)[None, :]
    c, s = unit(k1 * src, D)
    gather = np.concatenate([c, sign * s], axis=0)
    j = np.tile(np.arange(R), 8)[None, :]
    tc, ts = unit(k1 * j, N)
    k2 = np.arange(R)[:, None]
    jj = np.arange(R)[None, :]
    cc, ss = unit(k2 * jj, R)
    ss = sign * ss
    rows = []
    for part in range(2 if full else 1):
        for e in range(blocks):
            out = np.zeros((R, 2, 4, R))
            out[:, 0, e, :] = cc if part == 0 else ss
            out[:, 1, e, :] = -ss if part == 0 else cc
            rows.append(out.reshape(R, L))
    finish = np.concatenate(rows, axis=0)
    return (
        jnp.asarray(gather, F32).astype(BF16),
        jnp.asarray(tc, F32),
        jnp.asarray(sign * ts, F32),
        jnp.asarray(finish, F32).astype(BF16),
    )


def fourth(x, sign):
    (ar, ai), (br, bi), (cr, ci), (dr, di) = x
    t0r, t0i, t1r, t1i = ar + cr, ai + ci, ar - cr, ai - ci
    t2r, t2i, t3r, t3i = br + dr, bi + di, br - dr, bi - di
    if sign < 0:
        t3r, t3i = -t3r, -t3i
    return (
        (t0r + t2r, t0i + t2i),
        (t1r - t3i, t1i + t3r),
        (t0r - t2r, t0i - t2i),
        (t1r + t3i, t1i - t3r),
    )


def times(x, re, im):
    if abs(im) < 1e-12 and abs(re - 1.0) < 1e-12:
        return x
    a, b = x
    return (a * re - b * im, a * im + b * re)


def sixteenth(x, sign):
    inner = []
    for b in range(4):
        y = fourth([x[4 * a + b] for a in range(4)], sign)
        turned = []
        for c in range(4):
            angle = sign * 2.0 * math.pi * b * c / 16
            turned.append(times(y[c], math.cos(angle), math.sin(angle)))
        inner.append(turned)
    out = [None] * 16
    for c in range(4):
        z = fourth([inner[b][c] for b in range(4)], sign)
        for d in range(4):
            out[c + 4 * d] = z[d]
    return out


def nt_dot(a, b):
    return lax.dot_general(a, b, (((1,), (1,)), ((), ())), preferred_element_type=F32)


def blocks_in(x, gather, tc, ts, flip):
    both = jnp.dot(gather, x, preferred_element_type=F32)
    parts = []
    for h in range(2):
        a = both[:D, h * L:(h + 1) * L]
        b = both[D:, h * L:(h + 1) * L]
        u = a * tc - b * ts
        v = b * tc + a * ts
        parts.append((u + flip * pltpu.roll(v, 64, 1)).astype(BF16))
    return jnp.concatenate(parts, axis=0)


def lane_iota(rows):
    return lax.broadcasted_iota(jnp.int32, (rows, L), 1)


def hops(step):
    return min(step, 4 - step)


def far(kw, kg):
    return hops(kw // 4) + hops(kw % 4) + hops(kg // 2) + 0.5 * (kg % 2)


WIDE_STEPS = sorted(range(1, NW), key=lambda k: -far(k, 0))
GRP_STEPS = sorted(range(1, NG), key=lambda k: -far(0, k))
ALL_STEPS = sorted(
    [(kw, kg) for kw in range(NW) for kg in range(NG) if kw or kg], key=lambda k: -far(*k)
)


def around():
    w = lax.axis_index("wide")
    g = lax.axis_index("grp")
    y = [lax.rem(w // 4 + k, 4) for k in range(4)]
    z = [lax.rem(w % 4 + k, 4) for k in range(4)]
    x = [lax.rem(g // 2 + k, 4) for k in range(4)]
    c = [g % 2, 1 - g % 2]
    ws = [y[k // 4] * 4 + z[k % 4] for k in range(NW)]
    gs = [x[k // 2] * 2 + c[k % 2] for k in range(NG)]
    return w, g, ws, gs


def greet_all(ws, gs):
    barrier = pltpu.get_barrier_semaphore()
    for kw, kg in ALL_STEPS:
        pl.semaphore_signal(
            barrier, inc=1, device_id=(ws[kw], gs[kg]), device_id_type=MESH
        )
    return barrier


def spread_all(send, recv, ssem, rsem, ws, gs):
    me = ws[0] * NG + gs[0]
    pltpu.make_async_copy(send.at[me], recv.at[me], rsem).start()
    for kw, kg in ALL_STEPS:
        pltpu.make_async_remote_copy(
            send.at[ws[kw] * NG + gs[kg]], recv.at[me], ssem, rsem,
            device_id=(ws[kw], gs[kg]), device_id_type=MESH,
        ).start()
    pltpu.make_async_copy(recv, recv, rsem).wait()


def sent(buf, n, sem):
    pltpu.make_async_copy(buf.at[pl.ds(0, n)], buf.at[pl.ds(0, n)], sem).wait()


def rise_kernel(
    tiles, eta, phi, tw_c, tw_s, spread, gather, bt_c, bt_s, finish,
    phys, foot,
    tb, wide32, send, recv, send1, recv1, send2, recv2,
    ssem, rsem, ssem1, rsem1, ssem2, rsem2,
):
    w, g, ws, gs = around()
    me = w * NG + g
    barrier = greet_all(ws, gs)

    row = lax.broadcasted_iota(jnp.int32, (R, L), 0)
    lane = lane_iota(R)
    kx = me * R + row
    kx = jnp.where(kx >= N // 2, kx - N, kx).astype(F32) * (2.0 * math.pi / N)

    for f in range(3):
        x = []
        for n1 in range(16):
            cols = slice(n1 * L, (n1 + 1) * L)
            if f == 0:
                x.append((eta[0, :, cols].astype(F32), eta[1, :, cols].astype(F32)))
            else:
                if f == 1:
                    k = kx
                else:
                    base = n1 * L if n1 < 8 else n1 * L - N
                    k = (lane + base).astype(F32) * (2.0 * math.pi / N)
                x.append((-k * phi[1, :, cols].astype(F32), k * phi[0, :, cols].astype(F32)))
        y = sixteenth(x, 1)
        for k1 in range(16):
            c, s = tw_c[k1:k1 + 1, :], tw_s[k1:k1 + 1, :]
            a, b = y[k1]
            re = (a * c - b * s).astype(BF16)
            im = (a * s + b * c).astype(BF16)
            up = slice(f * R, (f + 1) * R)
            dn = slice(64 + f * R, 64 + (f + 1) * R)
            tb[k1, up, 0:L] = re
            tb[k1, up, L:2 * L] = -im
            tb[k1, dn, 0:L] = im
            tb[k1, dn, L:2 * L] = re

    zero = jnp.zeros((R, 2 * L), BF16)

    def rows_out(kk, carry):
        for h in range(2):
            tb[2 * kk + h, 48:64, :] = zero
            tb[2 * kk + h, 112:128, :] = zero
        rhs = tb[pl.ds(2 * kk, 2)].reshape(2 * L, 2 * L)
        z = nt_dot(spread[...], rhs)
        wide32[pl.ds(2 * kk, D, stride=R), :] = z[:, :L]
        wide32[pl.ds(2 * kk + 1, D, stride=R), :] = z[:, L:]
        return carry

    lax.fori_loop(0, 8, rows_out, 0, unroll=2)

    def narrow(i, carry):
        part = wide32[pl.ds(pl.multiple_of(i * 128, 128), 128), :]
        send[pl.ds(i * 8, 8)] = part.reshape(8, R, L).astype(BF16)
        return carry

    lax.fori_loop(0, 16, narrow, 0)

    pl.semaphore_wait(barrier, D - 1)
    spread_all(send, recv, ssem, rsem, ws, gs)

    def widen(i, carry):
        part = recv[pl.ds(i * 8, 8)].astype(F32)
        wide32[pl.ds(pl.multiple_of(i * 128, 128), 128), :] = part.reshape(128, L)
        return carry

    lax.fori_loop(0, 16, widen, 0)

    flip = jnp.where(lane_iota(D) < 64, -1.0, 1.0).astype(F32)

    def columns(yy, carry):
        x = jnp.concatenate(
            [
                wide32[pl.ds(2 * yy, D, stride=R), :].astype(BF16),
                wide32[pl.ds(2 * yy + 1, D, stride=R), :].astype(BF16),
            ],
            axis=1,
        )
        t = blocks_in(x, gather[...], bt_c[...], bt_s[...], flip)
        out = nt_dot(finish[...], t)
        phys[pl.ds(2 * yy, 48, stride=R), :] = out[:, :L]
        phys[pl.ds(2 * yy + 1, 48, stride=R), :] = out[:, L:]
        return carry

    lax.fori_loop(0, 8, columns, 0, unroll=4)

    low = lane < 64

    def by_group(q, carry):
        for h in range(2):
            at = [pl.multiple_of((f * 16 + 2 * q + h) * R, R) for f in range(3)]
            ht = phys[pl.ds(at[0], R), :]
            vx = phys[pl.ds(at[1], R), :]
            vy = phys[pl.ds(at[2], R), :]
            send1[q, h] = ht.astype(BF16)
            send1[q, 2 + 2 * h] = jnp.where(low, vx, pltpu.roll(vy, 64, 1)).astype(BF16)
            send1[q, 3 + 2 * h] = jnp.where(low, pltpu.roll(vx, 64, 1), vy).astype(BF16)
        return carry

    lax.fori_loop(0, NG, by_group, 0, unroll=2)

    pltpu.make_async_copy(send1.at[g], recv1.at[g], rsem1).start()
    for k in GRP_STEPS:
        d = gs[k]
        pltpu.make_async_remote_copy(
            send1.at[d], recv1.at[g], ssem1, rsem1, device_id=(w, d), device_id_type=MESH
        ).start()
    pltpu.make_async_copy(recv1, recv1, rsem1).wait()

    def choose(d, carry):
        t0 = tiles[g * 32 + d]
        t1 = tiles[g * 32 + 16 + d]
        t = jnp.where(lax.shift_right_logical(t0, 6) == w, t0, t1)
        upper = jnp.bitwise_and(lax.shift_right_logical(t, 5), 1) * 4
        col = jnp.bitwise_and(t, 3)
        odd = jnp.bitwise_and(t, 1)
        pair = lax.shift_right_logical(col, 1)
        right = (lane * 0 + odd) == 1
        for q in range(4):
            send2[d, q] = recv1[upper + q, 2 + col]
        for q in range(2):
            a = recv1[upper + 2 * q, pair].astype(F32)
            b = recv1[upper + 2 * q + 1, pair].astype(F32)
            lo = jnp.where(right, pltpu.roll(a, 64, 1), a)
            hi = jnp.where(right, b, pltpu.roll(b, 64, 1))
            send2[d, 4 + q] = jnp.where(low, lo, hi).astype(BF16)
        return carry

    lax.fori_loop(0, NW, choose, 0)

    pltpu.make_async_copy(send2.at[w], recv2.at[w], rsem2).start()
    for k in WIDE_STEPS:
        d = ws[k]
        pltpu.make_async_remote_copy(
            send2.at[d], recv2.at[w], ssem2, rsem2, device_id=(d, g), device_id_type=MESH
        ).start()
    pltpu.make_async_copy(recv2, recv2, rsem2).wait()

    for s in range(2):
        t = tiles[g * 32 + s * 16 + w]
        band = jnp.bitwise_and(lax.shift_right_logical(t, 6), NW - 1)
        for q in range(6):
            foot[s, q] = recv2[band, q]

    sent(send, D - 1, ssem)
    sent(send1, NG - 1, ssem1)
    sent(send2, NW - 1, ssem2)


def patch_tables():
    pos = np.arange(SIDE)
    edge = np.minimum(pos, SIDE - 1 - pos)
    dist = np.minimum(edge[:, None], edge[None, :])
    weight = 0.3 + 0.7 * np.exp(-8.0 * dist / SIDE)
    x = np.arange(SIDE)
    pick = np.zeros((2, L, SIDE))
    for h in range(2):
        pick[h, 64 * h + x // 2, x] = 1.0
    rows = np.zeros((SIDE, TS))
    rows[x, x // 2] = 1.0
    halves = np.zeros((2, SIDE, 32))
    for i in range(SIDE):
        r = i // 2
        blk, within = r // 16, r % 16
        halves[blk % 2, i, (blk // 2) * 16 + within] = 1.0
    z = Z_BOTTOM + (np.arange(LV) + 0.5) * ((Z_TOP - Z_BOTTOM) / LV)
    prof = np.exp(DECAY_RATE * (z - Z_TOP))
    return (
        jnp.asarray(prof, F32),
        jnp.asarray(weight, F32),
        jnp.asarray(pick, F32).astype(BF16),
        jnp.asarray(rows, F32).astype(BF16),
        jnp.asarray(halves, F32).astype(BF16),
    )


RB = 16
PAD = 8
CHUNK = 16
TOGETHER = 8
BAND = 32


def rank_of(tiles, q, want):
    at = jnp.int32(0)
    for step in (16, 8, 4, 2, 1):
        at = at + jnp.where(tiles[q * 32 + at + step - 1] < want, step, 0)
    return at


def fall_kernel(
    tiles, prof, phys, foot, state, weight, pick, rows, halves, down_rows, down_cols,
    tw_c, tw_s, spread,
    state_out, landed, sea_out,
    source, st, hh, cf, bl, cm, got, tb, send, recv,
    in_sem, out_sem, csem, gsem, ssem, rsem,
):
    def fetch(s, i):
        part = pl.ds(i * CHUNK, CHUNK)
        return pltpu.make_async_copy(state.at[s, part], st.at[s, part], in_sem.at[s, i])

    def put(s, r):
        part = pl.ds(r * BAND, BAND)
        return pltpu.make_async_copy(
            st.at[s, :, part], state_out.at[s, :, part], out_sem.at[s, r]
        )

    for s in range(2):
        for i in range(LV // CHUNK):
            fetch(s, i).start()

    w, g, ws, gs = around()
    me = w * NG + g
    barrier = greet_all(ws, gs)

    scale = LV / (Z_TOP - Z_BOTTOM)
    lane = lax.broadcasted_iota(jnp.int32, (SIDE, SIDE), 1)
    sub = lax.broadcasted_iota(jnp.int32, (SIDE, SIDE), 0)

    def up(m, sel, spread_rows):
        wide = jnp.dot(m, sel, preferred_element_type=F32).astype(BF16)
        return jnp.dot(spread_rows, wide, preferred_element_type=F32)

    def faces(a, axis, index):
        after = jnp.where(index == SIDE - 1, a, pltpu.roll(a, SIDE - 1, axis))
        before = jnp.where(index == 0, a, pltpu.roll(a, 1, axis))
        return (0.5 * COURANT) * (a + after), (0.5 * COURANT) * (before + a)

    edge = jnp.zeros((LV, PAD, SIDE), F32)
    for s in range(2):
        vel = foot[s, 0:4].reshape(64, L)
        hgt = foot[s, 4:6].reshape(32, L)
        height = up(hgt, pick[0], halves[0]) + up(hgt, pick[1], halves[1])
        ax = up(vel, pick[0], rows[...])
        ay = up(vel, pick[1], rows[...])
        hh[s] = height * scale - Z_BOTTOM * scale
        center = jnp.zeros((SIDE, SIDE), F32)
        for n, (a, axis, index) in enumerate(((ax, 1, lane), (ay, 0, sub))):
            upper, lower = faces(a, axis, index)
            center += jnp.maximum(upper, 0.0) - jnp.minimum(lower, 0.0)
            from_up = jnp.minimum(upper, 0.0)
            from_low = -jnp.maximum(lower, 0.0)
            last, first = index == SIDE - 1, index == 0
            center += jnp.where(last, from_up, 0.0) + jnp.where(first, from_low, 0.0)
            cf[s, 1 + 2 * n] = jnp.where(last, 0.0, from_up)
            cf[s, 2 + 2 * n] = jnp.where(first, 0.0, from_low)
        cf[s, 0] = center
        bl[s, :, 0:PAD, :] = edge
        bl[s, :, PAD + SIDE:, :] = edge

    for q in range(NG):
        want = (2 * w + g // 4) * 32 + 4 * q
        at = rank_of(tiles, q, want)
        for c in range(4):
            found = tiles[q * 32 + at]
            source[0, 4 * q + c] = jnp.bitwise_and(at, NW - 1) * NG + q
            source[1, 4 * q + c] = lax.shift_right_logical(at, 4)
            source[2, 4 * q + c] = jnp.where(found == want + c, 1, 0)
            at = jnp.minimum(at + jnp.where(found <= want + c, 1, 0), 31)

    for s in range(2):
        for i in range(LV // CHUNK):
            fetch(s, i).wait()

            def blend(o, carry, s=s, i=i):
                for b in range(SIDE // RB):
                    rs = slice(b * RB, (b + 1) * RB)
                    h, wt = hh[s, rs, :], weight[rs, :]
                    keep = 1.0 - wt
                    for l in range(TOGETHER):
                        k = i * CHUNK + o * TOGETHER + l
                        under = jnp.clip(h - lax.convert_element_type(k, F32), 0.0, 1.0)
                        bl[s, k, PAD + b * RB:PAD + (b + 1) * RB, :] = (
                            wt * under + keep * st[s, k, rs, :].astype(F32)
                        )
                return carry

            lax.fori_loop(0, CHUNK // TOGETHER, blend, 0)

    high = lax.Precision.HIGHEST
    for r in range(SIDE // BAND):
        block = jnp.zeros((R, L), F32)
        for s in range(2):

            def move(o, accs, s=s, r=r):
                accs = list(accs)
                for n in range(BAND // RB):
                    first_row = r * BAND + n * RB
                    rs = slice(first_row, first_row + RB)
                    at = PAD + first_row
                    c0, c1, c2, c3, c4 = (cf[s, m, rs, :] for m in range(5))
                    for l in range(TOGETHER):
                        k = o * TOGETHER + l
                        mid = bl[s, k, at:at + RB, :]
                        nxt = bl[s, k, at + 1:at + 1 + RB, :]
                        prv = bl[s, k, at - 1:at - 1 + RB, :]
                        flow = c0 * mid + c1 * pltpu.roll(mid, SIDE - 1, 1)
                        flow = flow + c2 * pltpu.roll(mid, 1, 1) + c3 * nxt + c4 * prv
                        new = jnp.clip(mid - prof[k] * flow, 0.0, 1.0)
                        st[s, k, rs, :] = new.astype(BF16)
                        accs[n] = accs[n] + new
                return tuple(accs)

            none = jnp.zeros((RB, SIDE), F32)
            accs = lax.fori_loop(0, LV // TOGETHER, move, (none,) * (BAND // RB))
            put(s, r).start()
            column = jnp.concatenate(accs, axis=0) * (1.0 / scale) + Z_BOTTOM
            part = jnp.dot(down_rows[...], column, preferred_element_type=F32, precision=high)
            block += jnp.dot(part, down_cols[s], preferred_element_type=F32, precision=high)
        cm[r] = (0.25 * block).astype(BF16)

        if r == 0:
            pl.semaphore_wait(barrier, D - 1)
        for to in (r, r + 4):
            for kw in WIDE_STEPS + [0]:

                def post(to=to, kw=kw, r=r):
                    pltpu.make_async_remote_copy(
                        cm.at[r], got.at[me], csem, gsem,
                        device_id=(ws[kw], to), device_id_type=MESH,
                    ).start()

                if kw:
                    post()
                else:
                    pl.when(g != to)(post)

                    @pl.when(g == to)
                    def _(r=r):
                        pltpu.make_async_copy(cm.at[r], got.at[me], gsem).start()

    pltpu.make_async_copy(got, got, gsem).wait()

    lane = lane_iota(R)
    low = lane < 64
    x = []
    for k2 in range(16):
        sides = []
        for h in range(2):
            cc = 2 * k2 + h
            tile = got[source[0, cc]].astype(F32)
            same = (lane * 0 + source[1, cc]) == h
            sides.append(jnp.where(same, tile, pltpu.roll(tile, 64, 1)))
        there = jnp.where(low, source[2, 2 * k2], source[2, 2 * k2 + 1]) == 1
        ht = phys[k2 * R:(k2 + 1) * R, :]
        vx = phys[256 + k2 * R:256 + (k2 + 1) * R, :]
        vy = phys[512 + k2 * R:512 + (k2 + 1) * R, :]
        sea = jnp.where(there, jnp.where(low, sides[0], sides[1]), ht)
        sea_out[:, k2 * L:(k2 + 1) * L] = sea
        x.append((-(sea + 0.5 * (vx * vx + vy * vy)), jnp.zeros((R, L), F32)))
    y = sixteenth(x, -1)
    for k1 in range(16):
        c, s = tw_c[k1:k1 + 1, :], tw_s[k1:k1 + 1, :]
        a, b = y[k1]
        re = (a * c - b * s).astype(BF16)
        im = (a * s + b * c).astype(BF16)
        q, e = k1 // 4, k1 % 4
        up_rows = slice(e * R, (e + 1) * R)
        dn_rows = slice(64 + e * R, 64 + (e + 1) * R)
        tb[q, up_rows, 0:L] = re
        tb[q, up_rows, L:2 * L] = -im
        tb[q, dn_rows, 0:L] = im
        tb[q, dn_rows, L:2 * L] = re

    for q in range(2):
        rhs = tb[2 * q:2 * q + 2].reshape(2 * L, 2 * L)
        z = nt_dot(spread[...], rhs)
        send[:, 2 * q, :] = z[:, :L]
        send[:, 2 * q + 1, :] = z[:, L:]

    spread_all(send, recv, ssem, rsem, ws, gs)
    for q in range(4):
        landed[q] = recv[:, q, :].astype(BF16)

    sent(got, D - 1, csem)
    sent(send, D - 1, ssem)
    for s in range(2):
        for r in range(SIDE // BAND):
            put(s, r).wait()


def settle_kernel(
    landed, sea, state, gather, bt_c, bt_s, finish,
    surface, state_out, tendency,
    out32, held, in_sem, out_sem,
):
    def copy(i, source, target, sem):
        s, part = i // 4, pl.ds((i % 4) * CHUNK, CHUNK)
        return pltpu.make_async_copy(source.at[s, part], target.at[s, part], sem.at[i])

    for i in range(8):
        copy(i, state, held, in_sem).start()
    surface[...] = sea[...]

    for i in range(8):
        copy(i, state, held, in_sem).wait()
        copy(i, held, state_out, out_sem).start()

    flip = jnp.where(lane_iota(D) < 64, -1.0, 1.0).astype(F32)
    for q in range(2):
        xx = jnp.concatenate([landed[2 * q], landed[2 * q + 1]], axis=1)
        t = blocks_in(xx, gather[...], bt_c[...], bt_s[...], flip)
        done = nt_dot(finish[...], t) * (1.0 / N)
        for h in range(2):
            for c in range(2):
                for e in range(4):
                    r0 = (c * 4 + e) * R
                    out32[pl.ds(c * 256 + 8 * q + 4 * h + e, R, stride=R), :] = done[
                        r0:r0 + R, h * L:(h + 1) * L
                    ]
    for c in range(2):
        for k2 in range(16):
            at = c * 256 + k2 * R
            tendency[c, :, k2 * L:(k2 + 1) * L] = out32[at:at + R, :]

    for i in range(8):
        copy(i, held, state_out, out_sem).wait()


def vmem(n):
    return [pl.BlockSpec(memory_space=pltpu.VMEM)] * n


def shards(eta_hat, phi_hat, patch_tiles, fraction):
    smem = pl.BlockSpec(memory_space=pltpu.SMEM)
    dma = pltpu.SemaphoreType.DMA
    phys, foot = pl.pallas_call(
        rise_kernel,
        out_shape=(
            jax.ShapeDtypeStruct((48 * R, L), F32),
            jax.ShapeDtypeStruct((2, 6, R, L), BF16),
        ),
        in_specs=[smem] + vmem(9),
        out_specs=tuple(vmem(2)),
        scratch_shapes=[
            pltpu.VMEM((16, L, 2 * L), BF16),
            pltpu.VMEM((D * R, L), F32),
            pltpu.VMEM((D, R, L), BF16),
            pltpu.VMEM((D, R, L), BF16),
            pltpu.VMEM((NG, 6, R, L), BF16),
            pltpu.VMEM((NG, 6, R, L), BF16),
            pltpu.VMEM((NW, 6, R, L), BF16),
            pltpu.VMEM((NW, 6, R, L), BF16),
        ] + [dma] * 6,
        compiler_params=pltpu.CompilerParams(
            collective_id=1, has_side_effects=True, vmem_limit_bytes=VMEM_LIMIT
        ),
        name="rise",
    )(patch_tiles, eta_hat, phi_hat, *lane_tables(1), *block_tables(1, 3, False))

    prof, weight, pick, rows, halves = patch_tables()
    down_rows = jnp.swapaxes(rows[:BAND, :R], 0, 1).astype(F32)
    down_cols = jnp.swapaxes(pick, 1, 2).astype(F32)
    anywhere = pl.BlockSpec(memory_space=pl.ANY)
    new_state, landed, sea = pl.pallas_call(
        fall_kernel,
        out_shape=(
            jax.ShapeDtypeStruct((2, LV, SIDE, SIDE), BF16),
            jax.ShapeDtypeStruct((4, D, L), BF16),
            jax.ShapeDtypeStruct((R, N), F32),
        ),
        in_specs=[smem, smem] + vmem(2) + [anywhere] + vmem(9),
        out_specs=(anywhere,) + tuple(vmem(2)),
        scratch_shapes=[
            pltpu.SMEM((3, 32), jnp.int32),
            pltpu.VMEM((2, LV, SIDE, SIDE), BF16),
            pltpu.VMEM((2, SIDE, SIDE), F32),
            pltpu.VMEM((2, 5, SIDE, SIDE), F32),
            pltpu.VMEM((2, LV, SIDE + 2 * PAD, SIDE), F32),
            pltpu.VMEM((4, R, L), BF16),
            pltpu.VMEM((D, R, L), BF16),
            pltpu.VMEM((4, L, 2 * L), BF16),
            pltpu.VMEM((D, 4, L), F32),
            pltpu.VMEM((D, 4, L), F32),
            dma((2, LV // CHUNK)),
            dma((2, SIDE // BAND)),
        ] + [dma] * 4,
        compiler_params=pltpu.CompilerParams(
            collective_id=2, has_side_effects=True, vmem_limit_bytes=VMEM_LIMIT
        ),
        name="fall",
    )(
        patch_tiles, prof, phys, foot, fraction[:, 0], weight, pick, rows, halves,
        down_rows, down_cols, *lane_tables(-1),
    )

    surface, new_state, tendency = pl.pallas_call(
        settle_kernel,
        out_shape=(
            jax.ShapeDtypeStruct((R, N), F32),
            jax.ShapeDtypeStruct((2, LV, SIDE, SIDE), BF16),
            jax.ShapeDtypeStruct((2, R, N), F32),
        ),
        in_specs=vmem(2) + [anywhere] + vmem(4),
        out_specs=(vmem(1)[0], anywhere, vmem(1)[0]),
        scratch_shapes=[
            pltpu.VMEM((512, L), F32),
            pltpu.VMEM((2, LV, SIDE, SIDE), BF16),
            dma((8,)),
            dma((8,)),
        ],
        compiler_params=pltpu.CompilerParams(vmem_limit_bytes=VMEM_LIMIT),
        name="settle",
    )(landed, sea, new_state, *block_tables(-1, 4, True))
    return (surface, new_state[:, None], tendency)


def solution(mesh):
    placed = (
        P(None, ("wide", "grp"), None),
        P(None, ("wide", "grp"), None),
        P(),
        P(None, ("wide", "grp"), None, None, None),
    )
    return jax.shard_map(
        shards,
        mesh=mesh,
        in_specs=placed,
        out_specs=(
            P(("wide", "grp"), None),
            P(None, ("wide", "grp"), None, None, None),
            P(None, ("wide", "grp"), None),
        ),
        check_vma=False,
    )
```

time: 103 us -> 73.3 us (0.71)
  Pallas kernels: 99.3 us -> 72.5 us
  local copies, waits for them, and re-layouts: 3.24 us -> 0 us
    pallas_call x2, Pallas kernels: 59.5 us -> 37.1 us  [the longest x1 31.7 us: shards(): pl.pallas_call(fall_kernel, out_shape=(jax.ShapeDtypeStruct((2, LV, SIDE,...]
    pallas_call x1, Pallas kernels: 39.7 us -> 35.4 us  [shards(): pl.pallas_call(rise_kernel, out_shape=(jax.ShapeDtypeStruct((48 * R, L),...]
    unnamed x2 -> x0, local copies, waits for them, and re-layouts: 3.24 us -> none
where the time goes in v3:
time: 73.3 us; the launch traced here: 73.1 us
  Pallas kernels  72.5 us (99%)
    pallas_call x1, Pallas kernels, shards(): pl.pallas_call(rise_kernel, out_shape=(jax.ShapeDtypeStruct((48 * R, L),...  35.4 us
    pallas_call x1, Pallas kernels, shards(): pl.pallas_call(fall_kernel, out_shape=(jax.ShapeDtypeStruct((2, LV, SIDE,...  31.7 us
    pallas_call x1, Pallas kernels, shards(): pl.pallas_call(settle_kernel, out_shape=(jax.ShapeDtypeStruct((R, N), F32...  5.36 us

profile of v3, /device:TPU:1, one launch (start us, length us, event | category | flops | bytes accessed | tf_op | source)
XLA Modules:
  0.0 73.1 jit_solution(6287521260925615637)
XLA Ops:
  0.6 35.4 %rise.1 = (f32[768,128]{1,0:T(8,128)}, bf16[2,6,16,128]{3,2,1,0:T(8,128)(2,1)}) custom-call(s32[256]{0:T(256)} %tiles.3, bf16[2,16,2048]{2,1,0:T(8,128)(2,1)} %eta.1, bf16[2,16,2048]{2,1,0:T(8,128)(2,1)} %phi.1, f32[16,128]{1,0:T(8,128)} %constant.34.clone.tw_c, f32[16,128]{1,0:T(8,128)} %constant.35.clone.tw_s, bf16[128,256]{1,0:T(8,128)(2,1)} %constant.54.spread, ...), custom_call_target="tpu_custom_call" | custom-call | tf_op jit(solution)/shard_map/rise/pallas_call | solution.py:617
  36.0 31.7 %fall.1 = (bf16[2,64,128,128]{3,2,1,0:T(8,128)(2,1)}, bf16[4,128,128]{2,1,0:T(8,128)(2,1)}, f32[16,2048]{1,0:T(8,128)}) custom-call(s32[256]{0:T(256)} %tiles.3, f32[64]{0:T(128)} %constant.41.clone.prof, f32[768,128]{1,0:T(8,128)} %get-tuple-element.11.phys, bf16[2,6,16,128]{3,2,1,0:T(8,128)(2,1)} %get-tuple-element.12.foot, ...), custom_call_target="tpu_custom_call" | custom-call | tf_op jit(solution)/shard_map/fall/pallas_call | solution.py:645
  67.7 5.4 %settle.1 = (f32[16,2048]{1,0:T(8,128)}, bf16[2,64,128,128]{3,2,1,0:T(8,128)(2,1)}, f32[2,16,2048]{2,1,0:T(8,128)}) custom-call(bf16[4,128,128]{2,1,0:T(8,128)(2,1)} %get-tuple-element.13.landed, f32[16,2048]{1,0:T(8,128)} %get-tuple-element.14.sea, bf16[2,64,128,128]{3,2,1,0:T(8,128)(2,1)} %get-tuple-element.15.state, bf16[256,128]{1,0:T(8,128)(2,1)} %constant.66.gather, ...), custom_call_target="tpu_custom_call" | custom-call | tf_op jit(solution)/shard_map/settle/pallas_call | solution.py:677

commit v4 on v3

--- a/solution.py
+++ b/solution.py
@@ -177,164 +177,32 @@
             send.at[ws[kw] * NG + gs[kg]], recv.at[me], ssem, rsem,
             device_id=(ws[kw], gs[kg]), device_id_type=MESH,
         ).start()
-    pltpu.make_async_copy(recv, recv, rsem).wait()
+
+
+def spread_grp(send, recv, ssem, rsem, ws, gs):
+    pltpu.make_async_copy(send.at[gs[0]], recv.at[gs[0]], rsem).start()
+    for k in GRP_STEPS:
+        pltpu.make_async_remote_copy(
+            send.at[gs[k]], recv.at[gs[0]], ssem, rsem,
+            device_id=(ws[0], gs[k]), device_id_type=MESH,
+        ).start()
+
+
+def spread_wide(send, recv, ssem, rsem, ws, gs):
+    pltpu.make_async_copy(send.at[ws[0]], recv.at[ws[0]], rsem).start()
+    for k in WIDE_STEPS:
+        pltpu.make_async_remote_copy(
+            send.at[ws[k]], recv.at[ws[0]], ssem, rsem,
+            device_id=(ws[k], gs[0]), device_id_type=MESH,
+        ).start()
+
+
+def landed_all(buf, sem):
+    pltpu.make_async_copy(buf, buf, sem).wait()
 
 
 def sent(buf, n, sem):
     pltpu.make_async_copy(buf.at[pl.ds(0, n)], buf.at[pl.ds(0, n)], sem).wait()
-
-
-def rise_kernel(
-    tiles, eta, phi, tw_c, tw_s, spread, gather, bt_c, bt_s, finish,
-    phys, foot,
-    tb, wide32, send, recv, send1, recv1, send2, recv2,
-    ssem, rsem, ssem1, rsem1, ssem2, rsem2,
-):
-    w, g, ws, gs = around()
-    me = w * NG + g
-    barrier = greet_all(ws, gs)
-
-    row = lax.broadcasted_iota(jnp.int32, (R, L), 0)
-    lane = lane_iota(R)
-    kx = me * R + row
-    kx = jnp.where(kx >= N // 2, kx - N, kx).astype(F32) * (2.0 * math.pi / N)
-
-    for f in range(3):
-        x = []
-        for n1 in range(16):
-            cols = slice(n1 * L, (n1 + 1) * L)
-            if f == 0:
-                x.append((eta[0, :, cols].astype(F32), eta[1, :, cols].astype(F32)))
-            else:
-                if f == 1:
-                    k = kx
-                else:
-                    base = n1 * L if n1 < 8 else n1 * L - N
-                    k = (lane + base).astype(F32) * (2.0 * math.pi / N)
-                x.append((-k * phi[1, :, cols].astype(F32), k * phi[0, :, cols].astype(F32)))
-        y = sixteenth(x, 1)
-        for k1 in range(16):
-            c, s = tw_c[k1:k1 + 1, :], tw_s[k1:k1 + 1, :]
-            a, b = y[k1]
-            re = (a * c - b * s).astype(BF16)
-            im = (a * s + b * c).astype(BF16)
-            up = slice(f * R, (f + 1) * R)
-            dn = slice(64 + f * R, 64 + (f + 1) * R)
-            tb[k1, up, 0:L] = re
-            tb[k1, up, L:2 * L] = -im
-            tb[k1, dn, 0:L] = im
-            tb[k1, dn, L:2 * L] = re
-
-    zero = jnp.zeros((R, 2 * L), BF16)
-
-    def rows_out(kk, carry):
-        for h in range(2):
-            tb[2 * kk + h, 48:64, :] = zero
-            tb[2 * kk + h, 112:128, :] = zero
-        rhs = tb[pl.ds(2 * kk, 2)].reshape(2 * L, 2 * L)
-        z = nt_dot(spread[...], rhs)
-        wide32[pl.ds(2 * kk, D, stride=R), :] = z[:, :L]
-        wide32[pl.ds(2 * kk + 1, D, stride=R), :] = z[:, L:]
-        return carry
-
-    lax.fori_loop(0, 8, rows_out, 0, unroll=2)
-
-    def narrow(i, carry):
-        part = wide32[pl.ds(pl.multiple_of(i * 128, 128), 128), :]
-        send[pl.ds(i * 8, 8)] = part.reshape(8, R, L).astype(BF16)
-        return carry
-
-    lax.fori_loop(0, 16, narrow, 0)
-
-    pl.semaphore_wait(barrier, D - 1)
-    spread_all(send, recv, ssem, rsem, ws, gs)
-
-    def widen(i, carry):
-        part = recv[pl.ds(i * 8, 8)].astype(F32)
-        wide32[pl.ds(pl.multiple_of(i * 128, 128), 128), :] = part.reshape(128, L)
-        return carry
-
-    lax.fori_loop(0, 16, widen, 0)
-
-    flip = jnp.where(lane_iota(D) < 64, -1.0, 1.0).astype(F32)
-
-    def columns(yy, carry):
-        x = jnp.concatenate(
-            [
-                wide32[pl.ds(2 * yy, D, stride=R), :].astype(BF16),
-                wide32[pl.ds(2 * yy + 1, D, stride=R), :].astype(BF16),
-            ],
-            axis=1,
-        )
-        t = blocks_in(x, gather[...], bt_c[...], bt_s[...], flip)
-        out = nt_dot(finish[...], t)
-        phys[pl.ds(2 * yy, 48, stride=R), :] = out[:, :L]
-        phys[pl.ds(2 * yy + 1, 48, stride=R), :] = out[:, L:]
-        return carry
-
-    lax.fori_loop(0, 8, columns, 0, unroll=4)
-
-    low = lane < 64
-
-    def by_group(q, carry):
-        for h in range(2):
-            at = [pl.multiple_of((f * 16 + 2 * q + h) * R, R) for f in range(3)]
-            ht = phys[pl.ds(at[0], R), :]
-            vx = phys[pl.ds(at[1], R), :]
-            vy = phys[pl.ds(at[2], R), :]
-            send1[q, h] = ht.astype(BF16)
-            send1[q, 2 + 2 * h] = jnp.where(low, vx, pltpu.roll(vy, 64, 1)).astype(BF16)
-            send1[q, 3 + 2 * h] = jnp.where(low, pltpu.roll(vx, 64, 1), vy).astype(BF16)
-        return carry
-
-    lax.fori_loop(0, NG, by_group, 0, unroll=2)
-
-    pltpu.make_async_copy(send1.at[g], recv1.at[g], rsem1).start()
-    for k in GRP_STEPS:
-        d = gs[k]
-        pltpu.make_async_remote_copy(
-            send1.at[d], recv1.at[g], ssem1, rsem1, device_id=(w, d), device_id_type=MESH
-        ).start()
-    pltpu.make_async_copy(recv1, recv1, rsem1).wait()
-
-    def choose(d, carry):
-        t0 = tiles[g * 32 + d]
-        t1 = tiles[g * 32 + 16 + d]
-        t = jnp.where(lax.shift_right_logical(t0, 6) == w, t0, t1)
-        upper = jnp.bitwise_and(lax.shift_right_logical(t, 5), 1) * 4
-        col = jnp.bitwise_and(t, 3)
-        odd = jnp.bitwise_and(t, 1)
-        pair = lax.shift_right_logical(col, 1)
-        right = (lane * 0 + odd) == 1
-        for q in range(4):
-            send2[d, q] = recv1[upper + q, 2 + col]
-        for q in range(2):
-            a = recv1[upper + 2 * q, pair].astype(F32)
-            b = recv1[upper + 2 * q + 1, pair].astype(F32)
-            lo = jnp.where(right, pltpu.roll(a, 64, 1), a)
-            hi = jnp.where(right, b, pltpu.roll(b, 64, 1))
-            send2[d, 4 + q] = jnp.where(low, lo, hi).astype(BF16)
-        return carry
-
-    lax.fori_loop(0, NW, choose, 0)
-
-    pltpu.make_async_copy(send2.at[w], recv2.at[w], rsem2).start()
-    for k in WIDE_STEPS:
-        d = ws[k]
-        pltpu.make_async_remote_copy(
-            send2.at[d], recv2.at[w], ssem2, rsem2, device_id=(d, g), device_id_type=MESH
-        ).start()
-    pltpu.make_async_copy(recv2, recv2, rsem2).wait()
-
-    for s in range(2):
-        t = tiles[g * 32 + s * 16 + w]
-        band = jnp.bitwise_and(lax.shift_right_logical(t, 6), NW - 1)
-        for q in range(6):
-            foot[s, q] = recv2[band, q]
-
-    sent(send, D - 1, ssem)
-    sent(send1, NG - 1, ssem1)
-    sent(send2, NW - 1, ssem2)
 
 
 def patch_tables():
@@ -378,12 +246,15 @@
     return at
 
 
-def fall_kernel(
-    tiles, prof, phys, foot, state, weight, pick, rows, halves, down_rows, down_cols,
-    tw_c, tw_s, spread,
+def step_kernel(
+    tiles, prof, eta, phi, state, weight, pick, rows, halves, down_rows, down_cols,
+    up_c, up_s, up_spread, gather, bt_c, bt_s, finish, tw_c, tw_s, spread,
     state_out, landed, sea_out,
-    source, st, hh, cf, bl, cm, got, tb, send, recv,
-    in_sem, out_sem, csem, gsem, ssem, rsem,
+    source, tb_a, wide32, send_a, recv_a, phys,
+    send1h, recv1h, send1v, recv1v, send2h, recv2h, send2v, recv2v,
+    st, hh, cf, bl, cm, got, tb, send, recv,
+    in_sem, out_sem, asem, arsem, ssem1h, rsem1h, ssem1v, rsem1v,
+    ssem2h, rsem2h, ssem2v, rsem2v, csem, gsem, ssem, rsem,
 ):
     def fetch(s, i):
         part = pl.ds(i * CHUNK, CHUNK)
@@ -395,37 +266,224 @@
             st.at[s, :, part], state_out.at[s, :, part], out_sem.at[s, r]
         )
 
+    w, g, ws, gs = around()
+    me = w * NG + g
+    barrier = greet_all(ws, gs)
     for s in range(2):
         for i in range(LV // CHUNK):
             fetch(s, i).start()
 
-    w, g, ws, gs = around()
-    me = w * NG + g
-    barrier = greet_all(ws, gs)
-
+    row = lax.broadcasted_iota(jnp.int32, (R, L), 0)
+    lane = lane_iota(R)
+    kx = me * R + row
+    kx = jnp.where(kx >= N // 2, kx - N, kx).astype(F32) * (2.0 * math.pi / N)
+
+    for f in range(3):
+        x = []
+        for n1 in range(16):
+            cols = slice(n1 * L, (n1 + 1) * L)
+            if f == 0:
+                x.append((eta[0, :, cols].astype(F32), eta[1, :, cols].astype(F32)))
+            else:
+                if f == 1:
+                    k = kx
+                else:
+                    base = n1 * L if n1 < 8 else n1 * L - N
+                    k = (lane + base).astype(F32) * (2.0 * math.pi / N)
+                x.append((-k * phi[1, :, cols].astype(F32), k * phi[0, :, cols].astype(F32)))
+        y = sixteenth(x, 1)
+        for k1 in range(16):
+            c, s = up_c[k1:k1 + 1, :], up_s[k1:k1 + 1, :]
+            a, b = y[k1]
+            re = (a * c - b * s).astype(BF16)
+            im = (a * s + b * c).astype(BF16)
+            up = slice(f * R, (f + 1) * R)
+            dn = slice(64 + f * R, 64 + (f + 1) * R)
+            tb_a[k1, up, 0:L] = re
+            tb_a[k1, up, L:2 * L] = -im
+            tb_a[k1, dn, 0:L] = im
+            tb_a[k1, dn, L:2 * L] = re
+
+    zero = jnp.zeros((R, 2 * L), BF16)
+
+    def rows_out(kk, carry):
+        for h in range(2):
+            tb_a[2 * kk + h, 48:64, :] = zero
+            tb_a[2 * kk + h, 112:128, :] = zero
+        rhs = tb_a[pl.ds(2 * kk, 2)].reshape(2 * L, 2 * L)
+        z = nt_dot(up_spread[...], rhs)
+        wide32[pl.ds(2 * kk, D, stride=R), :] = z[:, :L]
+        wide32[pl.ds(2 * kk + 1, D, stride=R), :] = z[:, L:]
+        return carry
+
+    lax.fori_loop(0, 8, rows_out, 0, unroll=2)
+
+    def narrow(i, carry):
+        part = wide32[pl.ds(pl.multiple_of(i * 128, 128), 128), :]
+        send_a[pl.ds(i * 8, 8)] = part.reshape(8, R, L).astype(BF16)
+        return carry
+
+    lax.fori_loop(0, 16, narrow, 0)
+
+    pl.semaphore_wait(barrier, D - 1)
+    spread_all(send_a, recv_a, asem, arsem, ws, gs)
+
+    for q in range(NG):
+        want = (2 * w + g // 4) * 32 + 4 * q
+        at = rank_of(tiles, q, want)
+        for c in range(4):
+            found = tiles[q * 32 + at]
+            source[0, 4 * q + c] = jnp.bitwise_and(at, NW - 1) * NG + q
+            source[1, 4 * q + c] = lax.shift_right_logical(at, 4)
+            source[2, 4 * q + c] = jnp.where(found == want + c, 1, 0)
+            at = jnp.minimum(at + jnp.where(found <= want + c, 1, 0), 31)
+
+    edge = jnp.zeros((LV, PAD, SIDE), F32)
+    for s in range(2):
+        bl[s, :, 0:PAD, :] = edge
+        bl[s, :, PAD + SIDE:, :] = edge
+        for i in range(LV // CHUNK):
+            fetch(s, i).wait()
+
+        def share(o, carry, s=s):
+            for b in range(SIDE // RB):
+                rs = slice(b * RB, (b + 1) * RB)
+                keep = 1.0 - weight[rs, :]
+                for l in range(TOGETHER):
+                    k = o * TOGETHER + l
+                    bl[s, k, PAD + b * RB:PAD + (b + 1) * RB, :] = (
+                        keep * st[s, k, rs, :].astype(F32)
+                    )
+            return carry
+
+        lax.fori_loop(0, LV // TOGETHER, share, 0)
+
+    landed_all(recv_a, arsem)
+
+    def widen(i, carry):
+        part = recv_a[pl.ds(i * 8, 8)].astype(F32)
+        wide32[pl.ds(pl.multiple_of(i * 128, 128), 128), :] = part.reshape(128, L)
+        return carry
+
+    lax.fori_loop(0, 16, widen, 0)
+
+    flip = jnp.where(lane_iota(D) < 64, -1.0, 1.0).astype(F32)
+
+    def columns(yy, carry):
+        x = jnp.concatenate(
+            [
+                wide32[pl.ds(2 * yy, D, stride=R), :].astype(BF16),
+                wide32[pl.ds(2 * yy + 1, D, stride=R), :].astype(BF16),
+            ],
+            axis=1,
+        )
+        t = blocks_in(x, gather[...], bt_c[...], bt_s[...], flip)
+        out = nt_dot(finish[...], t)
+        phys[pl.ds(2 * yy, 48, stride=R), :] = out[:, :L]
+        phys[pl.ds(2 * yy + 1, 48, stride=R), :] = out[:, L:]
+        return carry
+
+    lax.fori_loop(0, 8, columns, 0, unroll=4)
+
+    low = lane < 64
+
+    def heights(q, carry):
+        for h in range(2):
+            at = pl.multiple_of((2 * q + h) * R, R)
+            send1h[q, h] = phys[pl.ds(at, R), :].astype(BF16)
+        return carry
+
+    lax.fori_loop(0, NG, heights, 0, unroll=4)
+    spread_grp(send1h, recv1h, ssem1h, rsem1h, ws, gs)
+
+    def speeds(q, carry):
+        for h in range(2):
+            vx = phys[pl.ds(pl.multiple_of((16 + 2 * q + h) * R, R), R), :]
+            vy = phys[pl.ds(pl.multiple_of((32 + 2 * q + h) * R, R), R), :]
+            send1v[q, 2 * h] = jnp.where(low, vx, pltpu.roll(vy, 64, 1)).astype(BF16)
+            send1v[q, 2 * h + 1] = jnp.where(low, pltpu.roll(vx, 64, 1), vy).astype(BF16)
+        return carry
+
+    lax.fori_loop(0, NG, speeds, 0, unroll=2)
+    spread_grp(send1v, recv1v, ssem1v, rsem1v, ws, gs)
+
+    def tile_for(d):
+        t0 = tiles[g * 32 + d]
+        t1 = tiles[g * 32 + 16 + d]
+        t = jnp.where(lax.shift_right_logical(t0, 6) == w, t0, t1)
+        return jnp.bitwise_and(lax.shift_right_logical(t, 5), 1) * 4, jnp.bitwise_and(t, 3)
+
+    landed_all(recv1h, rsem1h)
+
+    def choose_heights(d, carry):
+        upper, col = tile_for(d)
+        right = (lane * 0 + jnp.bitwise_and(col, 1)) == 1
+        pair = lax.shift_right_logical(col, 1)
+        for q in range(2):
+            a = recv1h[upper + 2 * q, pair].astype(F32)
+            b = recv1h[upper + 2 * q + 1, pair].astype(F32)
+            lo = jnp.where(right, pltpu.roll(a, 64, 1), a)
+            hi = jnp.where(right, b, pltpu.roll(b, 64, 1))
+            send2h[d, q] = jnp.where(low, lo, hi).astype(BF16)
+        return carry
+
+    lax.fori_loop(0, NW, choose_heights, 0, unroll=4)
+    spread_wide(send2h, recv2h, ssem2h, rsem2h, ws, gs)
+
+    landed_all(recv1v, rsem1v)
+
+    def choose_speeds(d, carry):
+        upper, col = tile_for(d)
+        for q in range(4):
+            send2v[d, q] = recv1v[upper + q, col]
+        return carry
+
+    lax.fori_loop(0, NW, choose_speeds, 0, unroll=4)
+    spread_wide(send2v, recv2v, ssem2v, rsem2v, ws, gs)
+
+    bands = [
+        jnp.bitwise_and(lax.shift_right_logical(tiles[g * 32 + s * 16 + w], 6), NW - 1)
+        for s in range(2)
+    ]
     scale = LV / (Z_TOP - Z_BOTTOM)
-    lane = lax.broadcasted_iota(jnp.int32, (SIDE, SIDE), 1)
-    sub = lax.broadcasted_iota(jnp.int32, (SIDE, SIDE), 0)
 
     def up(m, sel, spread_rows):
         wide = jnp.dot(m, sel, preferred_element_type=F32).astype(BF16)
         return jnp.dot(spread_rows, wide, preferred_element_type=F32)
+
+    landed_all(recv2h, rsem2h)
+    for s in range(2):
+        hgt = recv2h[bands[s]].reshape(32, L)
+        height = up(hgt, pick[0], halves[0]) + up(hgt, pick[1], halves[1])
+        hh[s] = height * scale - Z_BOTTOM * scale
+
+        def blend(o, carry, s=s):
+            for b in range(SIDE // RB):
+                rs = slice(b * RB, (b + 1) * RB)
+                h, wt = hh[s, rs, :], weight[rs, :]
+                for l in range(TOGETHER):
+                    k = o * TOGETHER + l
+                    under = jnp.clip(h - lax.convert_element_type(k, F32), 0.0, 1.0)
+                    bl[s, k, PAD + b * RB:PAD + (b + 1) * RB, :] += wt * under
+            return carry
+
+        lax.fori_loop(0, LV // TOGETHER, blend, 0)
+
+    across = lax.broadcasted_iota(jnp.int32, (SIDE, SIDE), 1)
+    sub = lax.broadcasted_iota(jnp.int32, (SIDE, SIDE), 0)
 
     def faces(a, axis, index):
         after = jnp.where(index == SIDE - 1, a, pltpu.roll(a, SIDE - 1, axis))
         before = jnp.where(index == 0, a, pltpu.roll(a, 1, axis))
         return (0.5 * COURANT) * (a + after), (0.5 * COURANT) * (before + a)
 
-    edge = jnp.zeros((LV, PAD, SIDE), F32)
+    landed_all(recv2v, rsem2v)
     for s in range(2):
-        vel = foot[s, 0:4].reshape(64, L)
-        hgt = foot[s, 4:6].reshape(32, L)
-        height = up(hgt, pick[0], halves[0]) + up(hgt, pick[1], halves[1])
+        vel = recv2v[bands[s]].reshape(64, L)
         ax = up(vel, pick[0], rows[...])
         ay = up(vel, pick[1], rows[...])
-        hh[s] = height * scale - Z_BOTTOM * scale
         center = jnp.zeros((SIDE, SIDE), F32)
-        for n, (a, axis, index) in enumerate(((ax, 1, lane), (ay, 0, sub))):
+        for n, (a, axis, index) in enumerate(((ax, 1, across), (ay, 0, sub))):
             upper, lower = faces(a, axis, index)
             center += jnp.maximum(upper, 0.0) - jnp.minimum(lower, 0.0)
             from_up = jnp.minimum(upper, 0.0)
@@ -435,37 +493,6 @@
             cf[s, 1 + 2 * n] = jnp.where(last, 0.0, from_up)
             cf[s, 2 + 2 * n] = jnp.where(first, 0.0, from_low)
         cf[s, 0] = center
-        bl[s, :, 0:PAD, :] = edge
-        bl[s, :, PAD + SIDE:, :] = edge
-
-    for q in range(NG):
-        want = (2 * w + g // 4) * 32 + 4 * q
-        at = rank_of(tiles, q, want)
-        for c in range(4):
-            found = tiles[q * 32 + at]
-            source[0, 4 * q + c] = jnp.bitwise_and(at, NW - 1) * NG + q
-            source[1, 4 * q + c] = lax.shift_right_logical(at, 4)
-            source[2, 4 * q + c] = jnp.where(found == want + c, 1, 0)
-            at = jnp.minimum(at + jnp.where(found <= want + c, 1, 0), 31)
-
-    for s in range(2):
-        for i in range(LV // CHUNK):
-            fetch(s, i).wait()
-
-            def blend(o, carry, s=s, i=i):
-                for b in range(SIDE // RB):
-                    rs = slice(b * RB, (b + 1) * RB)
-                    h, wt = hh[s, rs, :], weight[rs, :]
-                    keep = 1.0 - wt
-                    for l in range(TOGETHER):
-                        k = i * CHUNK + o * TOGETHER + l
-                        under = jnp.clip(h - lax.convert_element_type(k, F32), 0.0, 1.0)
-                        bl[s, k, PAD + b * RB:PAD + (b + 1) * RB, :] = (
-                            wt * under + keep * st[s, k, rs, :].astype(F32)
-                        )
-                return carry
-
-            lax.fori_loop(0, CHUNK // TOGETHER, blend, 0)
 
     high = lax.Precision.HIGHEST
     for r in range(SIDE // BAND):
@@ -499,8 +526,6 @@
             block += jnp.dot(part, down_cols[s], preferred_element_type=F32, precision=high)
         cm[r] = (0.25 * block).astype(BF16)
 
-        if r == 0:
-            pl.semaphore_wait(barrier, D - 1)
         for to in (r, r + 4):
             for kw in WIDE_STEPS + [0]:
 
@@ -519,10 +544,8 @@
                     def _(r=r):
                         pltpu.make_async_copy(cm.at[r], got.at[me], gsem).start()
 
-    pltpu.make_async_copy(got, got, gsem).wait()
-
-    lane = lane_iota(R)
-    low = lane < 64
+    landed_all(got, gsem)
+
     x = []
     for k2 in range(16):
         sides = []
@@ -559,9 +582,15 @@
         send[:, 2 * q + 1, :] = z[:, L:]
 
     spread_all(send, recv, ssem, rsem, ws, gs)
+    landed_all(recv, rsem)
     for q in range(4):
         landed[q] = recv[:, q, :].astype(BF16)
 
+    sent(send_a, D - 1, asem)
+    sent(send1h, NG - 1, ssem1h)
+    sent(send1v, NG - 1, ssem1v)
+    sent(send2h, NW - 1, ssem2h)
+    sent(send2v, NW - 1, ssem2v)
     sent(got, D - 1, csem)
     sent(send, D - 1, ssem)
     for s in range(2):
@@ -581,10 +610,6 @@
     for i in range(8):
         copy(i, state, held, in_sem).start()
     surface[...] = sea[...]
-
-    for i in range(8):
-        copy(i, state, held, in_sem).wait()
-        copy(i, held, state_out, out_sem).start()
 
     flip = jnp.where(lane_iota(D) < 64, -1.0, 1.0).astype(F32)
     for q in range(2):
@@ -598,6 +623,9 @@
                     out32[pl.ds(c * 256 + 8 * q + 4 * h + e, R, stride=R), :] = done[
                         r0:r0 + R, h * L:(h + 1) * L
                     ]
+        for i in range(4 * q, 4 * q + 4):
+            copy(i, state, held, in_sem).wait()
+            copy(i, held, state_out, out_sem).start()
     for c in range(2):
         for k2 in range(16):
             at = c * 256 + k2 * R
@@ -614,45 +642,34 @@
 def shards(eta_hat, phi_hat, patch_tiles, fraction):
     smem = pl.BlockSpec(memory_space=pltpu.SMEM)
     dma = pltpu.SemaphoreType.DMA
-    phys, foot = pl.pallas_call(
-        rise_kernel,
-        out_shape=(
-            jax.ShapeDtypeStruct((48 * R, L), F32),
-            jax.ShapeDtypeStruct((2, 6, R, L), BF16),
-        ),
-        in_specs=[smem] + vmem(9),
-        out_specs=tuple(vmem(2)),
-        scratch_shapes=[
-            pltpu.VMEM((16, L, 2 * L), BF16),
-            pltpu.VMEM((D * R, L), F32),
-            pltpu.VMEM((D, R, L), BF16),
-            pltpu.VMEM((D, R, L), BF16),
-            pltpu.VMEM((NG, 6, R, L), BF16),
-            pltpu.VMEM((NG, 6, R, L), BF16),
-            pltpu.VMEM((NW, 6, R, L), BF16),
-            pltpu.VMEM((NW, 6, R, L), BF16),
-        ] + [dma] * 6,
-        compiler_params=pltpu.CompilerParams(
-            collective_id=1, has_side_effects=True, vmem_limit_bytes=VMEM_LIMIT
-        ),
-        name="rise",
-    )(patch_tiles, eta_hat, phi_hat, *lane_tables(1), *block_tables(1, 3, False))
-
     prof, weight, pick, rows, halves = patch_tables()
     down_rows = jnp.swapaxes(rows[:BAND, :R], 0, 1).astype(F32)
     down_cols = jnp.swapaxes(pick, 1, 2).astype(F32)
     anywhere = pl.BlockSpec(memory_space=pl.ANY)
     new_state, landed, sea = pl.pallas_call(
-        fall_kernel,
+        step_kernel,
         out_shape=(
             jax.ShapeDtypeStruct((2, LV, SIDE, SIDE), BF16),
             jax.ShapeDtypeStruct((4, D, L), BF16),
             jax.ShapeDtypeStruct((R, N), F32),
         ),
-        in_specs=[smem, smem] + vmem(2) + [anywhere] + vmem(9),
+        in_specs=[smem, smem] + vmem(2) + [anywhere] + vmem(16),
         out_specs=(anywhere,) + tuple(vmem(2)),
         scratch_shapes=[
             pltpu.SMEM((3, 32), jnp.int32),
+            pltpu.VMEM((16, L, 2 * L), BF16),
+            pltpu.VMEM((D * R, L), F32),
+            pltpu.VMEM((D, R, L), BF16),
+            pltpu.VMEM((D, R, L), BF16),
+            pltpu.VMEM((48 * R, L), F32),
+            pltpu.VMEM((NG, 2, R, L), BF16),
+            pltpu.VMEM((NG, 2, R, L), BF16),
+            pltpu.VMEM((NG, 4, R, L), BF16),
+            pltpu.VMEM((NG, 4, R, L), BF16),
+            pltpu.VMEM((NW, 2, R, L), BF16),
+            pltpu.VMEM((NW, 2, R, L), BF16),
+            pltpu.VMEM((NW, 4, R, L), BF16),
+            pltpu.VMEM((NW, 4, R, L), BF16),
             pltpu.VMEM((2, LV, SIDE, SIDE), BF16),
             pltpu.VMEM((2, SIDE, SIDE), F32),
             pltpu.VMEM((2, 5, SIDE, SIDE), F32),
@@ -664,14 +681,14 @@
             pltpu.VMEM((D, 4, L), F32),
             dma((2, LV // CHUNK)),
             dma((2, SIDE // BAND)),
-        ] + [dma] * 4,
+        ] + [dma] * 14,
         compiler_params=pltpu.CompilerParams(
-            collective_id=2, has_side_effects=True, vmem_limit_bytes=VMEM_LIMIT
+            collective_id=1, has_side_effects=True, vmem_limit_bytes=VMEM_LIMIT
         ),
-        name="fall",
+        name="step",
     )(
-        patch_tiles, prof, phys, foot, fraction[:, 0], weight, pick, rows, halves,
-        down_rows, down_cols, *lane_tables(-1),
+        patch_tiles, prof, eta_hat, phi_hat, fraction[:, 0], weight, pick, rows, halves,
+        down_rows, down_cols, *lane_tables(1), *block_tables(1, 3, False), *lane_tables(-1),
     )
 
     surface, new_state, tendency = pl.pallas_call(

time: 73.3 us -> 67 us (0.914)
  Pallas kernels: 72.5 us -> 66.2 us
    pallas_call x2 -> x1, Pallas kernels: 67.1 us -> 60.8 us  [shards(): pl.pallas_call(step_kernel, out_shape=(jax.ShapeDtypeStruct((2, LV, SIDE,...]
where the time goes in v4:
time: 67 us; the launch traced here: 66.8 us
  Pallas kernels  66.2 us (99%)
    pallas_call x1, Pallas kernels, shards(): pl.pallas_call(step_kernel, out_shape=(jax.ShapeDtypeStruct((2, LV, SIDE,...  60.8 us
    pallas_call x1, Pallas kernels, shards(): pl.pallas_call(settle_kernel, out_shape=(jax.ShapeDtypeStruct((R, N), F32...  5.36 us

profile of v4, /device:TPU:1, one launch (start us, length us, event | category | flops | bytes accessed | tf_op | source)
XLA Modules:
  0.0 66.8 jit_solution(13257807015972421588)
XLA Ops:
  0.6 60.8 %step.1 = (bf16[2,64,128,128]{3,2,1,0:T(8,128)(2,1)}, bf16[4,128,128]{2,1,0:T(8,128)(2,1)}, f32[16,2048]{1,0:T(8,128)}) custom-call(s32[256]{0:T(256)} %tiles.1, f32[64]{0:T(128)} %constant.34.clone.prof, bf16[2,16,2048]{2,1,0:T(8,128)(2,1)} %eta.1, bf16[2,16,2048]{2,1,0:T(8,128)(2,1)} %phi.1, bf16[2,64,128,128]{3,2,1,0:T(8,128)(2,1)} %bitcast.4, ...), custom_call_target="tpu_custom_call" | custom-call | tf_op jit(solution)/shard_map/step/pallas_call | solution.py:649
  61.5 5.4 %settle.1 = (f32[16,2048]{1,0:T(8,128)}, bf16[2,64,128,128]{3,2,1,0:T(8,128)(2,1)}, f32[2,16,2048]{2,1,0:T(8,128)}) custom-call(bf16[4,128,128]{2,1,0:T(8,128)(2,1)} %get-tuple-element.9.landed, f32[16,2048]{1,0:T(8,128)} %get-tuple-element.10.sea, bf16[2,64,128,128]{3,2,1,0:T(8,128)(2,1)} %get-tuple-element.11.state, bf16[256,128]{1,0:T(8,128)(2,1)} %constant.66.gather, ...), custom_call_target="tpu_custom_call" | custom-call | tf_op jit(solution)/shard_map/settle/pallas_call | solution.py:694

commit v5 on v4

--- a/solution.py
+++ b/solution.py
@@ -236,6 +236,7 @@
 PAD = 8
 CHUNK = 16
 TOGETHER = 8
+LONG = 32
 BAND = 32
 
 
@@ -246,11 +247,26 @@
     return at
 
 
-def step_kernel(
-    tiles, prof, eta, phi, state, weight, pick, rows, halves, down_rows, down_cols,
-    up_c, up_s, up_spread, gather, bt_c, bt_s, finish, tw_c, tw_s, spread,
-    state_out, landed, sea_out,
-    source, tb_a, wide32, send_a, recv_a, phys,
+EARLY = 5
+
+
+def step_kernel(tiles, prof, state, *refs):
+    operands, refs = refs[:18], refs[18:]
+    state_out, landed_out, sea_out = refs[:3]
+    held, refs = refs[3:21], refs[21:]
+    load_sem, done_sem = refs[-2:]
+    step_body(
+        tiles, prof, state, state_out, landed_out, sea_out, operands, held, load_sem, done_sem,
+        *held, *refs[:-2]
+    )
+
+
+def step_body(
+    tiles, prof, state, state_out, landed_out, sea_out, operands, held, load_sem, done_sem,
+    eta, phi, up_c, up_s, up_spread,
+    weight, pick, rows, halves, down_rows, down_cols,
+    gather, bt_c, bt_s, finish, tw_c, tw_s, spread,
+    landed, sea_held, source, tb_a, wide32, send_a, recv_a, phys,
     send1h, recv1h, send1v, recv1v, send2h, recv2h, send2v, recv2v,
     st, hh, cf, bl, cm, got, tb, send, recv,
     in_sem, out_sem, asem, arsem, ssem1h, rsem1h, ssem1v, rsem1v,
@@ -266,12 +282,21 @@
             st.at[s, :, part], state_out.at[s, :, part], out_sem.at[s, r]
         )
 
+    def load(n):
+        return pltpu.make_async_copy(operands[n], held[n], load_sem.at[n])
+
+    for n in range(EARLY):
+        load(n).start()
     w, g, ws, gs = around()
     me = w * NG + g
     barrier = greet_all(ws, gs)
+    for n in range(EARLY, len(operands)):
+        load(n).start()
     for s in range(2):
         for i in range(LV // CHUNK):
             fetch(s, i).start()
+    for n in range(EARLY):
+        load(n).wait()
 
     row = lax.broadcasted_iota(jnp.int32, (R, L), 0)
     lane = lane_iota(R)
@@ -338,6 +363,8 @@
             source[2, 4 * q + c] = jnp.where(found == want + c, 1, 0)
             at = jnp.minimum(at + jnp.where(found <= want + c, 1, 0), 31)
 
+    for n in range(EARLY, len(operands)):
+        load(n).wait()
     edge = jnp.zeros((LV, PAD, SIDE), F32)
     for s in range(2):
         bl[s, :, 0:PAD, :] = edge
@@ -496,18 +523,18 @@
 
     high = lax.Precision.HIGHEST
     for r in range(SIDE // BAND):
-        block = jnp.zeros((R, L), F32)
-        for s in range(2):
-
-            def move(o, accs, s=s, r=r):
+
+        def slot(s, block, r=r):
+
+            def move(o, accs):
                 accs = list(accs)
                 for n in range(BAND // RB):
                     first_row = r * BAND + n * RB
                     rs = slice(first_row, first_row + RB)
                     at = PAD + first_row
                     c0, c1, c2, c3, c4 = (cf[s, m, rs, :] for m in range(5))
-                    for l in range(TOGETHER):
-                        k = o * TOGETHER + l
+                    for l in range(LONG):
+                        k = o * LONG + l
                         mid = bl[s, k, at:at + RB, :]
                         nxt = bl[s, k, at + 1:at + 1 + RB, :]
                         prv = bl[s, k, at - 1:at - 1 + RB, :]
@@ -519,12 +546,17 @@
                 return tuple(accs)
 
             none = jnp.zeros((RB, SIDE), F32)
-            accs = lax.fori_loop(0, LV // TOGETHER, move, (none,) * (BAND // RB))
-            put(s, r).start()
+            accs = lax.fori_loop(0, LV // LONG, move, (none,) * (BAND // RB))
             column = jnp.concatenate(accs, axis=0) * (1.0 / scale) + Z_BOTTOM
             part = jnp.dot(down_rows[...], column, preferred_element_type=F32, precision=high)
-            block += jnp.dot(part, down_cols[s], preferred_element_type=F32, precision=high)
+            return block + jnp.dot(
+                part, down_cols[s], preferred_element_type=F32, precision=high
+            )
+
+        block = lax.fori_loop(0, 2, slot, jnp.zeros((R, L), F32))
         cm[r] = (0.25 * block).astype(BF16)
+        for s in range(2):
+            put(s, r).start()
 
         for to in (r, r + 4):
             for kw in WIDE_STEPS + [0]:
@@ -559,7 +591,7 @@
         vx = phys[256 + k2 * R:256 + (k2 + 1) * R, :]
         vy = phys[512 + k2 * R:512 + (k2 + 1) * R, :]
         sea = jnp.where(there, jnp.where(low, sides[0], sides[1]), ht)
-        sea_out[:, k2 * L:(k2 + 1) * L] = sea
+        sea_held[:, k2 * L:(k2 + 1) * L] = sea
         x.append((-(sea + 0.5 * (vx * vx + vy * vy)), jnp.zeros((R, L), F32)))
     y = sixteenth(x, -1)
     for k1 in range(16):
@@ -582,9 +614,13 @@
         send[:, 2 * q + 1, :] = z[:, L:]
 
     spread_all(send, recv, ssem, rsem, ws, gs)
+    sea_done = pltpu.make_async_copy(sea_held, sea_out, done_sem.at[0])
+    sea_done.start()
     landed_all(recv, rsem)
     for q in range(4):
         landed[q] = recv[:, q, :].astype(BF16)
+    all_done = pltpu.make_async_copy(landed, landed_out, done_sem.at[1])
+    all_done.start()
 
     sent(send_a, D - 1, asem)
     sent(send1h, NG - 1, ssem1h)
@@ -596,20 +632,32 @@
     for s in range(2):
         for r in range(SIDE // BAND):
             put(s, r).wait()
-
-
-def settle_kernel(
-    landed, sea, state, gather, bt_c, bt_s, finish,
-    surface, state_out, tendency,
-    out32, held, in_sem, out_sem,
-):
+    sea_done.wait()
+    all_done.wait()
+
+
+def settle_kernel(*refs):
+    operands, (state,) = refs[:6], refs[6:7]
+    surface, state_out, tendency = refs[7:10]
+    held = refs[10:16]
+    landed, gather, bt_c, bt_s, finish, sea = held
+    out32, spectrum, kept, load_sem, done_sem, in_sem, out_sem = refs[16:]
+
     def copy(i, source, target, sem):
         s, part = i // 4, pl.ds((i % 4) * CHUNK, CHUNK)
         return pltpu.make_async_copy(source.at[s, part], target.at[s, part], sem.at[i])
 
+    loads = [
+        pltpu.make_async_copy(operands[n], held[n], load_sem.at[n]) for n in range(6)
+    ]
+    for n in range(6):
+        loads[n].start()
     for i in range(8):
-        copy(i, state, held, in_sem).start()
-    surface[...] = sea[...]
+        copy(i, state, kept, in_sem).start()
+    for n in range(6):
+        loads[n].wait()
+    sea_done = pltpu.make_async_copy(sea, surface, done_sem.at[0])
+    sea_done.start()
 
     flip = jnp.where(lane_iota(D) < 64, -1.0, 1.0).astype(F32)
     for q in range(2):
@@ -624,19 +672,19 @@
                         r0:r0 + R, h * L:(h + 1) * L
                     ]
         for i in range(4 * q, 4 * q + 4):
-            copy(i, state, held, in_sem).wait()
-            copy(i, held, state_out, out_sem).start()
+            copy(i, state, kept, in_sem).wait()
+            copy(i, kept, state_out, out_sem).start()
     for c in range(2):
         for k2 in range(16):
             at = c * 256 + k2 * R
-            tendency[c, :, k2 * L:(k2 + 1) * L] = out32[at:at + R, :]
+            spectrum[c, :, k2 * L:(k2 + 1) * L] = out32[at:at + R, :]
+    all_done = pltpu.make_async_copy(spectrum, tendency, done_sem.at[1])
+    all_done.start()
 
     for i in range(8):
-        copy(i, held, state_out, out_sem).wait()
-
-
-def vmem(n):
-    return [pl.BlockSpec(memory_space=pltpu.VMEM)] * n
+        copy(i, kept, state_out, out_sem).wait()
+    sea_done.wait()
+    all_done.wait()
 
 
 def shards(eta_hat, phi_hat, patch_tiles, fraction):
@@ -646,6 +694,10 @@
     down_rows = jnp.swapaxes(rows[:BAND, :R], 0, 1).astype(F32)
     down_cols = jnp.swapaxes(pick, 1, 2).astype(F32)
     anywhere = pl.BlockSpec(memory_space=pl.ANY)
+    operands = (
+        eta_hat, phi_hat, *lane_tables(1), weight, pick, rows, halves,
+        down_rows, down_cols, *block_tables(1, 3, False), *lane_tables(-1),
+    )
     new_state, landed, sea = pl.pallas_call(
         step_kernel,
         out_shape=(
@@ -653,9 +705,11 @@
             jax.ShapeDtypeStruct((4, D, L), BF16),
             jax.ShapeDtypeStruct((R, N), F32),
         ),
-        in_specs=[smem, smem] + vmem(2) + [anywhere] + vmem(16),
-        out_specs=(anywhere,) + tuple(vmem(2)),
-        scratch_shapes=[
+        in_specs=[smem, smem] + [anywhere] * (1 + len(operands)),
+        out_specs=(anywhere,) * 3,
+        scratch_shapes=[pltpu.VMEM(x.shape, x.dtype) for x in operands] + [
+            pltpu.VMEM((4, D, L), BF16),
+            pltpu.VMEM((R, N), F32),
             pltpu.SMEM((3, 32), jnp.int32),
             pltpu.VMEM((16, L, 2 * L), BF16),
             pltpu.VMEM((D * R, L), F32),
@@ -681,16 +735,14 @@
             pltpu.VMEM((D, 4, L), F32),
             dma((2, LV // CHUNK)),
             dma((2, SIDE // BAND)),
-        ] + [dma] * 14,
+        ] + [dma] * 14 + [dma((len(operands),)), dma((2,))],
         compiler_params=pltpu.CompilerParams(
             collective_id=1, has_side_effects=True, vmem_limit_bytes=VMEM_LIMIT
         ),
         name="step",
-    )(
-        patch_tiles, prof, eta_hat, phi_hat, fraction[:, 0], weight, pick, rows, halves,
-        down_rows, down_cols, *lane_tables(1), *block_tables(1, 3, False), *lane_tables(-1),
-    )
-
+    )(patch_tiles, prof, fraction[:, 0], *operands)
+
+    last = (landed, *block_tables(-1, 4, True), sea)
     surface, new_state, tendency = pl.pallas_call(
         settle_kernel,
         out_shape=(
@@ -698,17 +750,20 @@
             jax.ShapeDtypeStruct((2, LV, SIDE, SIDE), BF16),
             jax.ShapeDtypeStruct((2, R, N), F32),
         ),
-        in_specs=vmem(2) + [anywhere] + vmem(4),
-        out_specs=(vmem(1)[0], anywhere, vmem(1)[0]),
-        scratch_shapes=[
+        in_specs=[anywhere] * 7,
+        out_specs=(anywhere,) * 3,
+        scratch_shapes=[pltpu.VMEM(x.shape, x.dtype) for x in last] + [
             pltpu.VMEM((512, L), F32),
+            pltpu.VMEM((2, R, N), F32),
             pltpu.VMEM((2, LV, SIDE, SIDE), BF16),
+            dma((6,)),
+            dma((2,)),
             dma((8,)),
             dma((8,)),
         ],
         compiler_params=pltpu.CompilerParams(vmem_limit_bytes=VMEM_LIMIT),
         name="settle",
-    )(landed, sea, new_state, *block_tables(-1, 4, True))
+    )(*last, new_state)
     return (surface, new_state[:, None], tendency)
 
 

time: 67 us -> 62.6 us (0.934)
  Pallas kernels: 66.2 us -> 61.9 us
    pallas_call x1, Pallas kernels: 60.8 us -> 57 us  [shards(): pl.pallas_call(step_kernel, out_shape=(jax.ShapeDtypeStruct((2, LV, SIDE,...]
where the time goes in v5:
time: 62.6 us; the launch traced here: 62.5 us
  Pallas kernels  61.9 us (99%)
  between operations  0.64 us (1%)
    pallas_call x1, Pallas kernels, shards(): pl.pallas_call(step_kernel, out_shape=(jax.ShapeDtypeStruct((2, LV, SIDE,...  57 us
    pallas_call x1, Pallas kernels, shards(): pl.pallas_call(settle_kernel, out_shape=(jax.ShapeDtypeStruct((R, N), F32...  4.85 us

profile of v5, /device:TPU:1, one launch (start us, length us, event | category | flops | bytes accessed | tf_op | source)
XLA Modules:
  0.0 62.5 jit_solution(17608322951702306236)
XLA Ops:
  0.6 57.0 %step.1 = (bf16[2,64,128,128]{3,2,1,0:T(8,128)(2,1)}, bf16[4,128,128]{2,1,0:T(8,128)(2,1)}, f32[16,2048]{1,0:T(8,128)}) custom-call(s32[256]{0:T(256)} %tiles.1, f32[64]{0:T(128)} %constant.34.clone.prof, bf16[2,64,128,128]{3,2,1,0:T(8,128)(2,1)} %bitcast.4, bf16[2,16,2048]{2,1,0:T(8,128)(2,1)} %refs_0_.1, bf16[2,16,2048]{2,1,0:T(8,128)(2,1)} %refs_1_.1, ...), custom_call_target="tpu_custom_call" | custom-call | tf_op jit(solution)/shard_map/step/pallas_call | solution.py:701
  57.6 4.8 %settle.1 = (f32[16,2048]{1,0:T(8,128)}, bf16[2,64,128,128]{3,2,1,0:T(8,128)(2,1)}, f32[2,16,2048]{2,1,0:T(8,128)}) custom-call(bf16[4,128,128]{2,1,0:T(8,128)(2,1)} %get-tuple-element.9.refs_0_, bf16[256,128]{1,0:T(8,128)(2,1)} %constant.66.refs_1_, f32[128,128]{1,0:T(8,128)} %constant.43.clone.refs_12_.refs_2_, f32[128,128]{1,0:T(8,128)} %constant.49.clone.refs_3_, ...), custom_call_target="tpu_custom_call" | custom-call | tf_op jit(solution)/shard_map/settle/pallas_call | solution.py:746

commit v6 on v5

--- a/solution.py
+++ b/solution.py
@@ -236,7 +236,7 @@
 PAD = 8
 CHUNK = 16
 TOGETHER = 8
-LONG = 32
+LONG = 64
 BAND = 32
 
 
@@ -454,7 +454,7 @@
             send2h[d, q] = jnp.where(low, lo, hi).astype(BF16)
         return carry
 
-    lax.fori_loop(0, NW, choose_heights, 0, unroll=4)
+    lax.fori_loop(0, NW, choose_heights, 0, unroll=8)
     spread_wide(send2h, recv2h, ssem2h, rsem2h, ws, gs)
 
     landed_all(recv1v, rsem1v)
@@ -465,7 +465,7 @@
             send2v[d, q] = recv1v[upper + q, col]
         return carry
 
-    lax.fori_loop(0, NW, choose_speeds, 0, unroll=4)
+    lax.fori_loop(0, NW, choose_speeds, 0, unroll=16)
     spread_wide(send2v, recv2v, ssem2v, rsem2v, ws, gs)
 
     bands = [
@@ -659,21 +659,31 @@
     sea_done = pltpu.make_async_copy(sea, surface, done_sem.at[0])
     sea_done.start()
 
+    def hand_on(i):
+        copy(i, state, kept, in_sem).wait()
+        copy(i, kept, state_out, out_sem).start()
+
+    for i in range(4):
+        hand_on(i)
+
     flip = jnp.where(lane_iota(D) < 64, -1.0, 1.0).astype(F32)
-    for q in range(2):
-        xx = jnp.concatenate([landed[2 * q], landed[2 * q + 1]], axis=1)
-        t = blocks_in(xx, gather[...], bt_c[...], bt_s[...], flip)
-        done = nt_dot(finish[...], t) * (1.0 / N)
-        for h in range(2):
-            for c in range(2):
-                for e in range(4):
-                    r0 = (c * 4 + e) * R
-                    out32[pl.ds(c * 256 + 8 * q + 4 * h + e, R, stride=R), :] = done[
-                        r0:r0 + R, h * L:(h + 1) * L
-                    ]
-        for i in range(4 * q, 4 * q + 4):
-            copy(i, state, kept, in_sem).wait()
-            copy(i, kept, state_out, out_sem).start()
+    turned = [
+        blocks_in(
+            jnp.concatenate([landed[2 * q], landed[2 * q + 1]], axis=1),
+            gather[...], bt_c[...], bt_s[...], flip,
+        )
+        for q in range(2)
+    ]
+    done = nt_dot(finish[...], jnp.concatenate(turned, axis=0)) * (1.0 / N)
+    for h in range(4):
+        for c in range(2):
+            for e in range(4):
+                r0 = (c * 4 + e) * R
+                out32[pl.ds(c * 256 + 4 * h + e, R, stride=R), :] = done[
+                    r0:r0 + R, h * L:(h + 1) * L
+                ]
+    for i in range(4, 8):
+        hand_on(i)
     for c in range(2):
         for k2 in range(16):
             at = c * 256 + k2 * R

time: 62.6 us -> 61.6 us (0.984)
  Pallas kernels: 61.9 us -> 60.9 us
where the time goes in v6:
time: 61.6 us; the launch traced here: 61.5 us
  Pallas kernels  60.9 us (99%)
  between operations  0.64 us (1%)
    pallas_call x1, Pallas kernels, shards(): pl.pallas_call(step_kernel, out_shape=(jax.ShapeDtypeStruct((2, LV, SIDE,...  56.4 us
    pallas_call x1, Pallas kernels, shards(): pl.pallas_call(settle_kernel, out_shape=(jax.ShapeDtypeStruct((R, N), F32...  4.45 us

profile of v6, /device:TPU:1, one launch (start us, length us, event | category | flops | bytes accessed | tf_op | source)
XLA Modules:
  0.0 61.5 jit_solution(18066007891781906610)
XLA Ops:
  0.6 56.4 %step.1 = (bf16[2,64,128,128]{3,2,1,0:T(8,128)(2,1)}, bf16[4,128,128]{2,1,0:T(8,128)(2,1)}, f32[16,2048]{1,0:T(8,128)}) custom-call(s32[256]{0:T(256)} %tiles.1, f32[64]{0:T(128)} %constant.34.clone.prof, bf16[2,64,128,128]{3,2,1,0:T(8,128)(2,1)} %bitcast.4, bf16[2,16,2048]{2,1,0:T(8,128)(2,1)} %refs_0_.1, bf16[2,16,2048]{2,1,0:T(8,128)(2,1)} %refs_1_.1, ...), custom_call_target="tpu_custom_call" | custom-call | tf_op jit(solution)/shard_map/step/pallas_call | solution.py:711
  57.1 4.5 %settle.1 = (f32[16,2048]{1,0:T(8,128)}, bf16[2,64,128,128]{3,2,1,0:T(8,128)(2,1)}, f32[2,16,2048]{2,1,0:T(8,128)}) custom-call(bf16[4,128,128]{2,1,0:T(8,128)(2,1)} %get-tuple-element.9.refs_0_, bf16[256,128]{1,0:T(8,128)(2,1)} %constant.66.refs_1_, f32[128,128]{1,0:T(8,128)} %constant.43.clone.refs_12_.refs_2_, f32[128,128]{1,0:T(8,128)} %constant.49.clone.refs_3_, ...), custom_call_target="tpu_custom_call" | custom-call | tf_op jit(solution)/shard_map/settle/pallas_call | solution.py:756

commit v7 on v6

--- a/solution.py
+++ b/solution.py
@@ -236,7 +236,7 @@
 PAD = 8
 CHUNK = 16
 TOGETHER = 8
-LONG = 64
+LONG = 32
 BAND = 32
 
 
@@ -524,15 +524,15 @@
     high = lax.Precision.HIGHEST
     for r in range(SIDE // BAND):
 
-        def slot(s, block, r=r):
-
-            def move(o, accs):
-                accs = list(accs)
+        def move(o, accs, r=r):
+            accs = list(accs)
+            for s in range(2):
                 for n in range(BAND // RB):
                     first_row = r * BAND + n * RB
                     rs = slice(first_row, first_row + RB)
                     at = PAD + first_row
                     c0, c1, c2, c3, c4 = (cf[s, m, rs, :] for m in range(5))
+                    acc = accs[2 * s + n]
                     for l in range(LONG):
                         k = o * LONG + l
                         mid = bl[s, k, at:at + RB, :]
@@ -542,18 +542,23 @@
                         flow = flow + c2 * pltpu.roll(mid, 1, 1) + c3 * nxt + c4 * prv
                         new = jnp.clip(mid - prof[k] * flow, 0.0, 1.0)
                         st[s, k, rs, :] = new.astype(BF16)
-                        accs[n] = accs[n] + new
-                return tuple(accs)
-
-            none = jnp.zeros((RB, SIDE), F32)
-            accs = lax.fori_loop(0, LV // LONG, move, (none,) * (BAND // RB))
-            column = jnp.concatenate(accs, axis=0) * (1.0 / scale) + Z_BOTTOM
-            part = jnp.dot(down_rows[...], column, preferred_element_type=F32, precision=high)
-            return block + jnp.dot(
-                part, down_cols[s], preferred_element_type=F32, precision=high
-            )
-
-        block = lax.fori_loop(0, 2, slot, jnp.zeros((R, L), F32))
+                        acc = acc + new
+                    accs[2 * s + n] = acc
+            return tuple(accs)
+
+        none = jnp.zeros((RB, SIDE), F32)
+        accs = lax.fori_loop(0, LV // LONG, move, (none,) * 4)
+        slots = [
+            jnp.concatenate(accs[2 * s:2 * s + 2], axis=0) * (1.0 / scale) + Z_BOTTOM
+            for s in range(2)
+        ]
+        part = jnp.dot(
+            down_rows[...], jnp.concatenate(slots, axis=1),
+            preferred_element_type=F32, precision=high,
+        )
+        block = jnp.dot(
+            part, down_cols[...].reshape(2 * SIDE, L), preferred_element_type=F32, precision=high
+        )
         cm[r] = (0.25 * block).astype(BF16)
         for s in range(2):
             put(s, r).start()

time: 61.6 us -> 61.1 us (level)
  no operation moved by 1% of the time
where the time goes in v7:
time: 61.1 us; the launch traced here: 60.9 us
  Pallas kernels  60.3 us (99%)
  between operations  0.64 us (1%)
    pallas_call x1, Pallas kernels, shards(): pl.pallas_call(step_kernel, out_shape=(jax.ShapeDtypeStruct((2, LV, SIDE,...  55.8 us
    pallas_call x1, Pallas kernels, shards(): pl.pallas_call(settle_kernel, out_shape=(jax.ShapeDtypeStruct((R, N), F32...  4.45 us

profile of v7, /device:TPU:1, one launch (start us, length us, event | category | flops | bytes accessed | tf_op | source)
XLA Modules:
  0.0 60.9 jit_solution(11881516216186899522)
XLA Ops:
  0.6 55.8 %step.1 = (bf16[2,64,128,128]{3,2,1,0:T(8,128)(2,1)}, bf16[4,128,128]{2,1,0:T(8,128)(2,1)}, f32[16,2048]{1,0:T(8,128)}) custom-call(s32[256]{0:T(256)} %tiles.1, f32[64]{0:T(128)} %constant.34.clone.prof, bf16[2,64,128,128]{3,2,1,0:T(8,128)(2,1)} %bitcast.4, bf16[2,16,2048]{2,1,0:T(8,128)(2,1)} %refs_0_.1, bf16[2,16,2048]{2,1,0:T(8,128)(2,1)} %refs_1_.1, ...), custom_call_target="tpu_custom_call" | custom-call | tf_op jit(solution)/shard_map/step/pallas_call | solution.py:716
  56.5 4.5 %settle.1 = (f32[16,2048]{1,0:T(8,128)}, bf16[2,64,128,128]{3,2,1,0:T(8,128)(2,1)}, f32[2,16,2048]{2,1,0:T(8,128)}) custom-call(bf16[4,128,128]{2,1,0:T(8,128)(2,1)} %get-tuple-element.9.refs_0_, bf16[256,128]{1,0:T(8,128)(2,1)} %constant.66.refs_1_, f32[128,128]{1,0:T(8,128)} %constant.43.clone.refs_12_.refs_2_, f32[128,128]{1,0:T(8,128)} %constant.49.clone.refs_3_, ...), custom_call_target="tpu_custom_call" | custom-call | tf_op jit(solution)/shard_map/settle/pallas_call | solution.py:761
